TPU v7x, 256 devices: a whole 4x4x8 slice. The times are simulated.
256 devices in a mesh: zg: 16 (over y, z_hi), xy: 16 (over x, z_lo, core).
Axes of the slice: x: 4, y: 4, z: 8 (z_hi: 4, z_lo: 2; z = z_hi * 2 + z_lo), core: 2. Of those that a mesh axis runs over, the one named last changes fastest.
Arguments:
- start_field: float32 [192, 128, 1024], P('zg', 'xy'), may hold values from -6 to 6
- diffusivity: float32 [192, 128, 1024], P('zg', 'xy'), may hold values from 0.02 to 0.13
- tile_block: int32 [192, 128, 16], P('zg', 'xy'), may hold values from 0 to 4096, as said below
- block_material: int32 [4096], replicated, may hold values from 0 to 1
- material_coupling: float32 [2, 64, 64], replicated, as said below
Outputs:
- final_field: float32 [192, 128, 1024], P('zg', 'xy')
Inputs may be any that keep to these rules, and one draw needn't show every extreme that they name: `tile_block`: 0 marks a tile outside every inclusion; k > 0 names inclusion block k - 1. `block_material`: an index into material_coupling. `material_coupling`: each material's coupling among the 64 cells of a tile.
All inputs are finite; a program needn't handle non-finite values.
Results may differ from a plain program's by a relative error of at most 0.0003.
Values sent between devices are 32-bit elements; how exact they have to be, the bound alone decides.
No kernel may reach another device: no remote copies, remote signals or barrier semaphores. Data moves between devices by JAX's collectives and lax.ppermute only.
A program may use at most 64 MiB of HBM per device.

v0:
```python
import jax
import jax.numpy as jnp
from jax import lax
from jax.experimental import pallas as pl
from jax.experimental.pallas import tpu as pltpu
from jax.sharding import PartitionSpec as P

TILE = 64
STEPS = 8
PLANES = 12
OWN = 8
HALO = 8
ROWS = OWN + 2 * HALO
SUB = 8
LANES = 128
CHUNKS = 8
VMEM_LIMIT = 24 * 1024 * 1024


SIDE = 4
OWN_AT = HALO * SUB
OWN_ROWS = OWN * SUB
HALF = SIDE * SUB
EDGE_PLANES = (0, 1, 2, 3, 8, 9, 10, 11)
REST = 3 * SUB
NEAR = HALF + REST
CODES_AT = PLANES * NEAR
RENEWED = (3, 3, 2, 1, 4, 4, 4, 4, 1, 2, 3, 3)
RENEWED_AT = [SUB * sum(RENEWED[:plane]) for plane in range(PLANES + 1)]


def reach(level):
    margin = HALO - SIDE + 1 + level % SIDE
    return margin, ROWS - margin


def span(low, high):
    return pl.ds(low * SUB, (high - low) * SUB)


TRACE_AT = [0]
for _level in range(SIDE):
    _low, _high = reach(_level)
    TRACE_AT.append(TRACE_AT[-1] + (_high - _low) * SUB)


def trace_place(level):
    start = TRACE_AT[level % SIDE]
    return pl.ds(start, TRACE_AT[level % SIDE + 1] - start)


KEPT = [(level, plane) for level in range(6) for plane in sorted({level, level + 1, 10 - level, 11 - level})]
EARLY_KEPT = {pair: i for i, pair in enumerate(pair for pair in KEPT if pair[0] < SIDE)}
LATE_KEPT = {pair: i for i, pair in enumerate(pair for pair in KEPT if pair[0] >= SIDE)}


def span_sum(cells):
    lane = lax.broadcasted_iota(jnp.int32, (1, SUB, LANES), 2)
    row = lax.broadcasted_iota(jnp.int32, (1, SUB, LANES), 1)
    after = jnp.where(row == SUB - 1, 0.0, pltpu.roll(cells, SUB - 1, 1))
    before = jnp.where(row == 0, 0.0, pltpu.roll(cells, 1, 1))
    return pltpu.roll(jnp.where(lane == 0, after, cells), LANES - 1, 2) + pltpu.roll(
        jnp.where(lane == LANES - 1, before, cells), 1, 2
    )


def split_cells(values):
    high = values.astype(jnp.bfloat16)
    low = (values - high.astype(jnp.float32)).astype(jnp.bfloat16)
    return high, low


def weights(couple_ref):
    high, low = split_cells(couple_ref[...])
    return jnp.concatenate([high, high, low], axis=0)


def advance(src, dst, conduct, code, weight, first, count, low, high):
    rows = high - low
    at = pl.ds(low * SUB, rows * SUB)
    mid = pl.ds(first + 1, count)
    here = src[mid, at, :]
    around = (
        src[pl.ds(first, count), at, :]
        + src[pl.ds(first + 2, count), at, :]
        + src[mid, pl.ds((low - 1) * SUB, rows * SUB), :]
        + src[mid, pl.ds((low + 1) * SUB, rows * SUB), :]
    )
    along = span_sum(here.reshape(count * rows, SUB, LANES)).reshape(here.shape)
    flat = here.reshape(count * rows * SUB, LANES)
    near, rest = split_cells(flat)
    product = jnp.dot(
        jnp.concatenate([near, rest, near], axis=1), weight, preferred_element_type=jnp.float32
    )
    plane = pl.ds(first, count)
    marks = code[plane, at, :]
    penalty = jnp.where(
        marks == 1.0,
        product[:, :LANES].reshape(here.shape),
        jnp.where(marks == 2.0, product[:, LANES:].reshape(here.shape), 0.0),
    )
    dst[mid, at, :] = here + conduct[plane, at, :] * (around + along - 6.0 * here) - penalty


def advance_groups(src, dst, conduct, code, weight, groups, count, stride, low, high):
    for i in range(groups):
        advance(src, dst, conduct, code, weight, i * stride, count, low, high)


def inside(axis):
    place = lax.axis_index(axis)
    return place > 0, place < lax.axis_size(axis) - 1


def kept_if(flag, values):
    return jnp.where(flag, values, 0.0)


def odd_place(axis):
    return lax.axis_index(axis) % 2 == 1


def send(first, second, at, upward, downward, axis="xy"):
    odd = odd_place(axis)
    first[at] = jnp.where(odd, upward, downward)
    second[at] = jnp.where(odd, downward, upward)


def got(first, second, at, from_before, axis="xy"):
    return jnp.where(odd_place(axis) == from_before, second[at], first[at])


def spread(block, dst, offset, at_plane, planes=range(PLANES)):
    for plane in planes:
        for chunk in range(CHUNKS):
            dst[plane + at_plane, pl.ds(offset * SUB + chunk, OWN, stride=SUB), :] = block[
                plane, :, chunk * LANES : (chunk + 1) * LANES
            ]


def widened(codes):
    tile_of = lax.broadcasted_iota(jnp.int32, (LANES, CHUNKS * LANES), 0)
    cell_of = lax.broadcasted_iota(jnp.int32, (LANES, CHUNKS * LANES), 1)
    widen = jnp.where(tile_of == cell_of // TILE, 1.0, 0.0).astype(jnp.bfloat16)
    flat = codes.reshape(-1, LANES).astype(jnp.bfloat16)
    wide = jnp.dot(flat, widen, preferred_element_type=jnp.float32)
    return wide.reshape(codes.shape[0], OWN, CHUNKS * LANES)


def ghosts(src, low, high, from_below=None, from_above=None):
    at = span(low, high)
    if from_below is None:
        src[0, at, :] = src[1, at, :] * 0.6
        src[PLANES + 1, at, :] = src[PLANES, at, :] * 0.6
    else:
        src[0, at, :] = (from_below + 0.75 * src[1, at, :]) * 0.8
        src[PLANES + 1, at, :] = (from_above + 0.75 * src[PLANES, at, :]) * 0.8


def put_traces(src, first, second, level):
    at = span(*reach(level))
    place = trace_place(level)
    to_below = 0.75 * src[2, at, :] - 0.25 * src[1, at, :]
    to_above = 0.75 * src[PLANES - 1, at, :] - 0.25 * src[PLANES, at, :]
    send(first, second, place, to_above, to_below, "zg")


def prepare_kernel(
    start_field, diffusivity, tile_block, block_material,
    first, second, code,
    own_v, own_d, own_t, material, tiles, field, conduct, to_first, to_second, codes, arrived, left,
):
    half = PLANES // 2
    loads = [
        pltpu.make_async_copy(tile_block, own_t, arrived.at[0]),
        pltpu.make_async_copy(block_material, material, arrived.at[1]),
    ]
    for i, (source, target) in enumerate(((start_field, own_v), (diffusivity, own_d))):
        for part in range(2):
            at = pl.ds(part * half, half)
            loads.append(
                pltpu.make_async_copy(source.at[at], target.at[at], arrived.at[2 + 2 * i + part])
            )
    for load in loads:
        load.start()
    stores = []

    def leave(source, target):
        store = pltpu.make_async_copy(source, target, left.at[len(stores)])
        store.start()
        stores.append(store)

    loads[0].wait()
    loads[1].wait()
    tiles[...] = jnp.zeros(tiles.shape, jnp.int32)
    tiles[:, :, : own_t.shape[2]] = own_t[...]
    table = material[...]
    row = lax.broadcasted_iota(jnp.int32, (SUB, LANES), 0)
    bits = jnp.zeros((SUB, LANES), jnp.int32)
    for part in range(table.shape[0] // SUB):
        bits = bits + (table[part * SUB : (part + 1) * SUB] << (row + part * SUB))
    for shift in (4, 2, 1):
        bits = bits + pltpu.roll(bits, shift, 0)
    for plane in range(PLANES):
        block = tiles[plane]
        entry = jnp.maximum(block - 1, 0)
        word = jnp.take_along_axis(bits, entry & (LANES - 1), axis=1)
        kind = (word >> (entry >> 7)) & 1
        codes[plane] = jnp.where(block > 0, kind + 1, 0).astype(jnp.float32)
        send(
            to_first, to_second, pl.ds(CODES_AT + 3 * plane, 3),
            codes[plane, 5:, :], codes[plane, :3, :],
        )
    for packet in (to_first, to_second):
        packet[CODES_AT + 3 * PLANES :, :] = jnp.zeros((4, LANES), jnp.float32)
    leave(codes, code)
    for part in range(2):
        planes = range(part * half, part * half + half)
        loads[2 + part].wait()
        spread(own_v, field, 0, 0, planes)
        loads[4 + part].wait()
        spread(own_d, conduct, 0, 0, planes)
        for plane in planes:
            at = plane * NEAR
            send(to_first, to_second, pl.ds(at, HALF), field[plane, HALF:, :], field[plane, :HALF, :])
            send(
                to_first, to_second, pl.ds(at + HALF, REST),
                conduct[plane, OWN_ROWS - REST :, :], conduct[plane, :REST, :],
            )
        at = pl.ds(0, half * NEAR) if part == 0 else pl.ds(half * NEAR, first.shape[0] - half * NEAR)
        leave(to_first.at[at], first.at[at])
        leave(to_second.at[at], second.at[at])
    for store in stores:
        store.wait()


def own_kernel(start_field, diffusivity, code, even, factor, marks, wide):
    spread(start_field, even, HALO, 0)
    spread(diffusivity, factor, HALO, 0)
    wide[...] = widened(code[...])
    spread(wide, marks, HALO, 0)


def keep(src, kept, places, level):
    low, high = reach(level)
    at = span(low - 1, high + 1)
    for plane in range(PLANES):
        if (level, plane) in places:
            kept[places[level, plane], at, :] = src[plane + 1, at, :]


def first_kernel(
    near_first, near_second, field, conduct, code, couple,
    first, second, trace_first, trace_second, state, kept, factor, marks,
    even, odd, wide, codes,
):
    weight = weights(couple)
    has_left, has_right = inside("xy")
    own = pl.ds(OWN_AT, OWN_ROWS)
    for flag, from_left, offset, near_at, rest_at, place in (
        (has_left, True, 0, 4 * SUB, 5 * SUB, 5),
        (has_right, False, HALO + OWN, 16 * SUB, 16 * SUB, 0),
    ):
        def packet(at, size):
            return kept_if(flag, got(near_first, near_second, pl.ds(at, size), from_left))

        codes[...] = jnp.zeros(codes.shape, jnp.float32)
        for plane in range(PLANES):
            at = plane * NEAR
            even[plane + 1, pl.ds(near_at, HALF), :] = packet(at, HALF)
            factor[plane, pl.ds(rest_at, REST), :] = packet(at + HALF, REST)
            codes[plane, place : place + 3, :] = packet(CODES_AT + 3 * plane, 3)
        wide[...] = widened(codes[...])
        spread(wide, marks, offset, 0)
    even[1 : PLANES + 1, own, :] = field[:, own, :]
    factor[:, own, :] = conduct[:, own, :]
    marks[:, own, :] = code[:, own, :]
    buffers = (even, odd)
    for level in range(SIDE):
        src, dst = buffers[level % 2], buffers[1 - level % 2]
        put_traces(src, trace_first, trace_second, level)
        keep(src, kept, EARLY_KEPT, level)
        low, high = reach(level)
        ghosts(src, low, high)
        advance_groups(src, dst, factor, marks, weight, 3, 4, 4, low, high)
    state[...] = even[1 : PLANES + 1, OWN_AT : OWN_AT + OWN_ROWS, :]
    for plane in range(PLANES):
        rows = RENEWED[plane] * SUB
        send(
            first, second, pl.ds(RENEWED_AT[plane], rows),
            state[plane, OWN_ROWS - rows :, :], state[plane, :rows, :],
        )


def middle_kernel(
    first, second, state, factor, marks, couple,
    trace_first, trace_second, kept,
    even, odd,
):
    weight = weights(couple)
    has_left, has_right = inside("xy")
    for plane in range(PLANES):
        rows = RENEWED[plane] * SUB
        at = pl.ds(RENEWED_AT[plane], rows)
        even[plane + 1, pl.ds(5 * SUB, REST), :] = jnp.zeros((REST, LANES), jnp.float32)
        even[plane + 1, pl.ds(16 * SUB, REST), :] = jnp.zeros((REST, LANES), jnp.float32)
        even[plane + 1, pl.ds(OWN_AT, OWN_ROWS), :] = state[plane]
        even[plane + 1, pl.ds(OWN_AT - rows, rows), :] = kept_if(has_left, got(first, second, at, True))
        even[plane + 1, pl.ds(16 * SUB, rows), :] = kept_if(has_right, got(first, second, at, False))
    buffers = (even, odd)
    for level in range(SIDE, STEPS):
        src, dst = buffers[level % 2], buffers[1 - level % 2]
        put_traces(src, trace_first, trace_second, level)
        keep(src, kept, LATE_KEPT, level)
        if level == STEPS - 1:
            break
        low, high = reach(level)
        ghosts(src, low + 1, high - 1)
        count = STEPS - level
        advance_groups(src, dst, factor, marks, weight, 2, count, PLANES - count, low + 1, high - 1)
        if level == SIDE:
            advance(src, dst, factor, marks, weight, 5, 2, low, high)


def second_steps(levels, buffers, kept, places, trace_first, trace_second, factor, marks, weight):
    has_below, has_above = inside("zg")
    for level in levels:
        src, dst = buffers[level % 2], buffers[1 - level % 2]
        low, high = reach(level)
        for plane in range(PLANES):
            if (level, plane) in places:
                at = span(low - 1, high + 1)
                src[plane + 1, at, :] = kept[places[level, plane], at, :]
        place = trace_place(level)
        ghosts(
            src, low, high,
            kept_if(has_below, got(trace_first, trace_second, place, True, "zg")),
            kept_if(has_above, got(trace_first, trace_second, place, False, "zg")),
        )
        groups, count, stride = (2, level + 1, 11 - level) if level < 5 else (3, 4, 4)
        advance_groups(src, dst, factor, marks, weight, groups, count, stride, low, high)


def second_kernel(
    trace_first, trace_second, kept, factor, marks, couple,
    first, second, state,
    even, odd,
):
    second_steps(range(SIDE), (even, odd), kept, EARLY_KEPT, trace_first, trace_second, factor, marks, weights(couple))
    for i, plane in enumerate(EDGE_PLANES):
        state[i] = even[plane + 1, pl.ds(OWN_AT, OWN_ROWS), :]
        send(first, second, i, state[i, HALF:, :], state[i, :HALF, :])


def last_kernel(
    trace_first, trace_second, first, second, state, kept, factor, marks, couple,
    result,
    even, odd,
):
    has_left, has_right = inside("xy")
    for i, plane in enumerate(EDGE_PLANES):
        even[plane + 1, pl.ds(OWN_AT, OWN_ROWS), :] = state[i]
        even[plane + 1, pl.ds(OWN_AT - HALF, HALF), :] = kept_if(has_left, got(first, second, i, True))
        even[plane + 1, pl.ds(OWN_AT + OWN_ROWS, HALF), :] = kept_if(has_right, got(first, second, i, False))
    second_steps(
        range(SIDE, STEPS), (even, odd), kept, LATE_KEPT, trace_first, trace_second, factor, marks,
        weights(couple),
    )
    for plane in range(PLANES):
        for chunk in range(CHUNKS):
            result[plane, :, chunk * LANES : (chunk + 1) * LANES] = even[
                plane + 1, pl.ds(OWN_AT + chunk, OWN, stride=SUB), :
            ]


def shape(*dims):
    return jax.ShapeDtypeStruct(dims, jnp.float32)


VMEM = pl.BlockSpec(memory_space=pltpu.VMEM)
HBM = pl.BlockSpec(memory_space=pltpu.HBM)
FIELD = (PLANES, ROWS * SUB, LANES)
PADDED = (PLANES + 2, ROWS * SUB, LANES)
CELLS = (PLANES, OWN_ROWS, LANES)
TRACES = (TRACE_AT[-1], LANES)
WIDE = (PLANES, OWN, CHUNKS * LANES)
PACKET = (CODES_AT + 3 * PLANES + 4, LANES)
SHARE = (RENEWED_AT[-1], LANES)
EDGE_SHARE = (len(EDGE_PLANES), HALF, LANES)


def call(kernel, outs, scratch, *operands, place=VMEM, out_place=VMEM, limit=VMEM_LIMIT):
    return pl.pallas_call(
        kernel,
        out_shape=[shape(*dims) for dims in outs],
        in_specs=[place] * len(operands),
        out_specs=[out_place] * len(outs),
        scratch_shapes=scratch,
        compiler_params=pltpu.CompilerParams(vmem_limit_bytes=limit),
        name=kernel.__name__,
    )(*operands)


def scratch(*shapes):
    return [pltpu.VMEM(dims, jnp.float32) for dims in shapes]


def swap(first, second, axis):
    levels, lines = lax.axis_size("zg"), lax.axis_size("xy")
    count = lax.axis_size(axis)

    def device(along, other):
        return along * lines + other if axis == "zg" else other * lines + along

    shifted, pairs = [], []
    for other in range(levels * lines // count):
        shifted += [(device(i, other), device(i + 1, other)) for i in range(1, count - 1, 2)]
        pairs += [(device(i, other), device(i + 1, other)) for i in range(0, count, 2)]
        idle = other ^ 1 if axis == "zg" else other ^ 4
        if idle > other:
            shifted += [(device(i, other), device(i, idle)) for i in (0, count - 1)]
    return tuple(
        lax.ppermute(cells, ("zg", "xy"), pairing + [(j, i) for i, j in pairing])
        for cells, pairing in ((first, shifted), (second, pairs))
    )


def on_device(start_field, diffusivity, tile_block, block_material, material_coupling):
    turned = jnp.swapaxes(material_coupling, 1, 2)
    empty = jnp.zeros((TILE, TILE), jnp.float32)
    couple = jnp.concatenate(
        [jnp.block([[turned[kind], empty], [empty, turned[kind]]]) for kind in (0, 1)], axis=1
    )
    material = block_material.reshape(-1, LANES)
    first, second, code = call(
        prepare_kernel,
        [PACKET, PACKET, (PLANES, OWN, LANES)],
        scratch(start_field.shape, diffusivity.shape)
        + [
            pltpu.VMEM(tile_block.shape, jnp.int32),
            pltpu.VMEM(material.shape, jnp.int32),
            pltpu.VMEM((PLANES, OWN, LANES), jnp.int32),
        ]
        + scratch(CELLS, CELLS, PACKET, PACKET, (PLANES, OWN, LANES))
        + [pltpu.SemaphoreType.DMA((6,)), pltpu.SemaphoreType.DMA((5,))],
        start_field, diffusivity, tile_block, material,
        place=HBM,
        out_place=HBM,
        limit=56 * 1024 * 1024,
    )
    near = swap(first, second, "xy")
    field, conduct, code = call(
        own_kernel, [FIELD] * 3, scratch(WIDE), start_field, diffusivity, code
    )
    first, second, trace_first, trace_second, state, early_kept, factor, marks = call(
        first_kernel,
        [SHARE, SHARE, TRACES, TRACES, CELLS, (len(EARLY_KEPT), ROWS * SUB, LANES), FIELD, FIELD],
        scratch(PADDED, PADDED, WIDE, (PLANES, OWN, LANES)),
        *near, field, conduct, code, couple,
    )
    sides = swap(first, second, "xy")
    early = swap(trace_first, trace_second, "zg")
    trace_first, trace_second, late_kept = call(
        middle_kernel,
        [TRACES, TRACES, (len(LATE_KEPT), ROWS * SUB, LANES)],
        scratch(PADDED, PADDED),
        *sides, state, factor, marks, couple,
    )
    late = swap(trace_first, trace_second, "zg")
    first, second, state = call(
        second_kernel,
        [EDGE_SHARE, EDGE_SHARE, (len(EDGE_PLANES), OWN_ROWS, LANES)],
        scratch(PADDED, PADDED),
        *early, early_kept, factor, marks, couple,
    )
    sides = swap(first, second, "xy")
    (result,) = call(
        last_kernel,
        [start_field.shape],
        scratch(PADDED, PADDED),
        *late, *sides, state, late_kept, factor, marks, couple,
    )
    return result


def solution(mesh):
    return jax.shard_map(
        on_device,
        mesh=mesh,
        in_specs=(P("zg", "xy", None), P("zg", "xy", None), P("zg", "xy", None), P(), P()),
        out_specs=P("zg", "xy", None),
        check_vma=False,
    )
```

profile of v0, /device:TPU:30, one launch (start us, length us, event | category | flops | bytes accessed | tf_op | source)
XLA Modules:
  0.0 48.1 jit_solution(16451189645510285445)
XLA Ops:
  0.0 2.2 %prepare_kernel.1 = (f32[712,128]{1,0:T(8,128)}, f32[712,128]{1,0:T(8,128)}, f32[12,8,128]{2,1,0:T(8,128)}) custom-call(f32[12,8,1024]{2,1,0:T(8,128)} %start_field.3, f32[12,8,1024]{2,1,0:T(8,128)} %diffusivity.3, s32[12,8,16]{2,1,0:T(8,128)} %tile_block.1, s32[32,128]{1,0:T(8,128)} %bitcast.7), custom_call_target="tpu_custom_call" | custom-call | tf_op jit(solution)/shard_map/prepare_kernel/pallas_call | solution.py:393
  2.2 1.7 %collective-permute-start = (f32[712,128]{1,0:T(8,128)}, f32[712,128]{1,0:T(8,128)S(1)}, u32[]{:S(2)}, u32[]{:S(2)}) collective-permute-start(f32[712,128]{1,0:T(8,128)} %get-tuple-element.25), channel_id=1, source_target_pairs={{1,2},{3,4},{5,6},{7,8},{9,10},{11,12},{13,14},{0,64},{15,79},{17,... | collective-permute-start | bytes 1093640 | tf_op jit(solution)/shard_map/ppermute | solution.py:423
  4.0 0.4 collective-permute-start.1
  4.4 0.9 %copy.6 = f32[2,64,64]{1,2,0:T(8,128)S(1)} copy(f32[2,64,64]{2,1,0:T(8,128)} %param.9) | data formatting | bytes 65536 | tf_op args[4]
  5.3 0.8 %copy-done.2 = f32[12,8,128]{2,1,0:T(8,128)S(1)} copy-done((f32[12,8,128]{2,1,0:T(8,128)S(1)}, f32[12,8,128]{2,1,0:T(8,128)}, u32[]{:S(2)}) %copy-start.2) | copy-done | bytes 49176
  6.1 0.3 own_kernel.1
  6.5 0.1 fusion.couple
  6.5 7.5 %collective-permute-done.near_first = f32[712,128]{1,0:T(8,128)S(1)} collective-permute-done((f32[712,128]{1,0:T(8,128)}, f32[712,128]{1,0:T(8,128)S(1)}, u32[]{:S(2)}, u32[]{:S(2)}) %collective-permute-start) | collective-permute-done | bytes 364576 | tf_op jit(solution)/shard_map/ppermute | solution.py:423
  14.1 0.0 collective-permute-done.1.near_second
  14.1 2.4 %first_kernel.1 = (f32[272,128]{1,0:T(8,128)S(1)}, f32[272,128]{1,0:T(8,128)S(1)}, f32[352,128]{1,0:T(8,128)S(1)}, f32[352,128]{1,0:T(8,128)S(1)}, f32[12,64,128...) custom-call(f32[712,128]{1,0:T(8,128)S(1)} %collective-permute-done.near, ...), custom_call_target="tpu_custom_call" | custom-call | tf_op jit(solution)/shard_map/first_kernel/pallas_call | solution.py:393
  16.5 1.6 %collective-permute-start.2 = (f32[272,128]{1,0:T(8,128)S(1)}, f32[272,128]{1,0:T(8,128)S(1)}, u32[]{:S(2)}, u32[]{:S(2)}) collective-permute-start(f32[272,128]{1,0:T(8,128)S(1)} %get-tuple-element.31), channel_id=1, source_target_pairs={{1,2},{3,4},{5,6},{7,8},{9,10},{11,12},{13,14},{0,64},{15,79},{17,... | collective-permute-start | bytes 417800 | tf_op jit(solution)/shard_map/ppermute | solution.py:423
  18.1 5.6 %collective-permute-start.6 = (f32[352,128]{1,0:T(8,128)S(1)}, f32[352,128]{1,0:T(8,128)S(1)}, u32[]{:S(2)}, u32[]{:S(2)}) collective-permute-start(f32[352,128]{1,0:T(8,128)S(1)} %get-tuple-element.38), channel_id=1, source_target_pairs={{16,32},{48,64},{80,96},{112,128},{144,160},{176,192},{208,224},{0... | collective-permute-start | bytes 540680 | tf_op jit(solution)/shard_map/ppermute | solution.py:423
  23.7 1.3 %collective-permute-start.7 = (f32[352,128]{1,0:T(8,128)S(1)}, f32[352,128]{1,0:T(8,128)S(1)}, u32[]{:S(2)}, u32[]{:S(2)}) collective-permute-start(f32[352,128]{1,0:T(8,128)S(1)} %get-tuple-element.39), channel_id=1, source_target_pairs={{0,16},{32,48},{64,80},{96,112},{128,144},{160,176},{192,208},{224... | collective-permute-start | bytes 540680 | tf_op jit(solution)/shard_map/ppermute | solution.py:423
  25.0 1.0 %middle_kernel.1 = (f32[352,128]{1,0:T(8,128)S(1)}, f32[352,128]{1,0:T(8,128)S(1)}, f32[6,192,128]{2,1,0:T(8,128)S(1)}) custom-call(f32[272,128]{1,0:T(8,128)S(1)} %collective-permute-done.2.first, f32[272,128]{1,0:T(8,128)S(1)} %collective-permute-done.3.second, f32[12,64,128]{2,1,0:T(8,128)S(1)} %get-tuple-element.33.state, ...), custom_call_target="tpu_custom_call" | custom-call | tf_op jit(solution)/shard_map/middle_kernel/pallas_call | solution.py:393
  26.0 6.6 %collective-permute-start.4 = (f32[352,128]{1,0:T(8,128)S(1)}, f32[352,128]{1,0:T(8,128)S(1)}, u32[]{:S(2)}, u32[]{:S(2)}) collective-permute-start(f32[352,128]{1,0:T(8,128)S(1)} %get-tuple-element.36), channel_id=1, source_target_pairs={{16,32},{48,64},{80,96},{112,128},{144,160},{176,192},{208,224},{0... | collective-permute-start | bytes 540680 | tf_op jit(solution)/shard_map/ppermute | solution.py:423
  32.6 1.2 %collective-permute-start.5 = (f32[352,128]{1,0:T(8,128)S(1)}, f32[352,128]{1,0:T(8,128)S(1)}, u32[]{:S(2)}, u32[]{:S(2)}) collective-permute-start(f32[352,128]{1,0:T(8,128)S(1)} %get-tuple-element.37), channel_id=1, source_target_pairs={{0,16},{32,48},{64,80},{96,112},{128,144},{160,176},{192,208},{224... | collective-permute-start | bytes 540680 | tf_op jit(solution)/shard_map/ppermute | solution.py:423
  33.8 5.1 %collective-permute-done.6.trace_first = f32[352,128]{1,0:T(8,128)S(1)} collective-permute-done((f32[352,128]{1,0:T(8,128)S(1)}, f32[352,128]{1,0:T(8,128)S(1)}, u32[]{:S(2)}, u32[]{:S(2)}) %collective-permute-start.6) | collective-permute-done | bytes 180256 | tf_op jit(solution)/shard_map/ppermute | solution.py:423
  38.9 0.0 collective-permute-done.7.trace_second
  38.9 1.0 %second_kernel.1 = (f32[8,32,128]{2,1,0:T(8,128)S(1)}, f32[8,32,128]{2,1,0:T(8,128)S(1)}, f32[8,64,128]{2,1,0:T(8,128)S(1)}) custom-call(f32[352,128]{1,0:T(8,128)S(1)} %collective-permute-done.6.trace_first, f32[352,128]{1,0:T(8,128)S(1)} %collective-permute-done.7.trace_second, f32[16,192,128]{2,1,0:T(8,128)S(1)} %get-tuple-element.40.kept, ...), custom_call_target="tpu_custom_call" | custom-call | tf_op jit(solution)/shard_map/second_kernel/pallas_call | solution.py:393
  39.9 0.1 collective-permute-start.8
  40.0 0.1 collective-permute-start.9
  40.1 5.2 %collective-permute-done.8.first = f32[8,32,128]{2,1,0:T(8,128)S(1)} collective-permute-done((f32[8,32,128]{2,1,0:T(8,128)S(1)}, f32[8,32,128]{2,1,0:T(8,128)S(1)}, u32[]{:S(2)}, u32[]{:S(2)}) %collective-permute-start.8) | collective-permute-done | bytes 131104 | tf_op jit(solution)/shard_map/ppermute | solution.py:423
  45.3 0.0 collective-permute-done.9.second
  45.3 2.8 %last_kernel.1 = f32[12,8,1024]{2,1,0:T(8,128)} custom-call(f32[352,128]{1,0:T(8,128)S(1)} %collective-permute-done.4.trace_first, f32[352,128]{1,0:T(8,128)S(1)} %collective-permute-done.5.trace_second, f32[8,32,128]{2,1,0:T(8,128)S(1)} %collective-permute-done.8.first, f32[8,32,128]{2,1,0:T(8,128)S(1)} %collective-permute-done.9.second, ...), custom_call_target="tpu_custom_call" | custom-call | tf_op jit(solution)/shard_map/last_kernel/pallas_call | solution.py:393
  (11 shorter events, 0.0 us)
Async XLA Ops:
  0.0 5.3 %copy-start.1 = (f32[12,8,1024]{2,1,0:T(8,128)S(1)}, f32[12,8,1024]{2,1,0:T(8,128)}, u32[]{:S(2)}) copy-start(f32[12,8,1024]{2,1,0:T(8,128)} %diffusivity.3) | copy-start | bytes 1179652
  0.0 5.3 %copy-start = (f32[12,8,1024]{2,1,0:T(8,128)S(1)}, f32[12,8,1024]{2,1,0:T(8,128)}, u32[]{:S(2)}) copy-start(f32[12,8,1024]{2,1,0:T(8,128)} %start_field.3) | copy-start | bytes 1179652
  2.2 11.8 %collective-permute-start = (f32[712,128]{1,0:T(8,128)}, f32[712,128]{1,0:T(8,128)S(1)}, u32[]{:S(2)}, u32[]{:S(2)}) collective-permute-start(f32[712,128]{1,0:T(8,128)} %get-tuple-element.25), channel_id=1, source_target_pairs={{1,2},{3,4},{5,6},{7,8},{9,10},{11,12},{13,14},{0,64},{15,79},{17,... | collective-permute-start | bytes 1093640 | tf_op jit(solution)/shard_map/ppermute | solution.py:423
  4.0 10.1 %collective-permute-start.1 = (f32[712,128]{1,0:T(8,128)}, f32[712,128]{1,0:T(8,128)S(1)}, u32[]{:S(2)}, u32[]{:S(2)}) collective-permute-start(f32[712,128]{1,0:T(8,128)} %get-tuple-element.26), channel_id=1, source_target_pairs={{0,1},{2,3},{4,5},{6,7},{8,9},{10,11},{12,13},{14,15},{16,17},{18,... | collective-permute-start | bytes 1093640 | tf_op jit(solution)/shard_map/ppermute | solution.py:423
  5.3 0.8 %copy-start.2 = (f32[12,8,128]{2,1,0:T(8,128)S(1)}, f32[12,8,128]{2,1,0:T(8,128)}, u32[]{:S(2)}) copy-start(f32[12,8,128]{2,1,0:T(8,128)} %get-tuple-element.27.code) | copy-start | bytes 147460
  16.5 8.5 %collective-permute-start.2 = (f32[272,128]{1,0:T(8,128)S(1)}, f32[272,128]{1,0:T(8,128)S(1)}, u32[]{:S(2)}, u32[]{:S(2)}) collective-permute-start(f32[272,128]{1,0:T(8,128)S(1)} %get-tuple-element.31), channel_id=1, source_target_pairs={{1,2},{3,4},{5,6},{7,8},{9,10},{11,12},{13,14},{0,64},{15,79},{17,... | collective-permute-start | bytes 417800 | tf_op jit(solution)/shard_map/ppermute | solution.py:423
  18.1 6.9 %collective-permute-start.3 = (f32[272,128]{1,0:T(8,128)S(1)}, f32[272,128]{1,0:T(8,128)S(1)}, u32[]{:S(2)}, u32[]{:S(2)}) collective-permute-start(f32[272,128]{1,0:T(8,128)S(1)} %get-tuple-element.32), channel_id=1, source_target_pairs={{0,1},{2,3},{4,5},{6,7},{8,9},{10,11},{12,13},{14,15},{16,17},{18,... | collective-permute-start | bytes 417800 | tf_op jit(solution)/shard_map/ppermute | solution.py:423
  18.1 20.8 %collective-permute-start.6 = (f32[352,128]{1,0:T(8,128)S(1)}, f32[352,128]{1,0:T(8,128)S(1)}, u32[]{:S(2)}, u32[]{:S(2)}) collective-permute-start(f32[352,128]{1,0:T(8,128)S(1)} %get-tuple-element.38), channel_id=1, source_target_pairs={{16,32},{48,64},{80,96},{112,128},{144,160},{176,192},{208,224},{0... | collective-permute-start | bytes 540680 | tf_op jit(solution)/shard_map/ppermute | solution.py:423
  23.7 15.2 %collective-permute-start.7 = (f32[352,128]{1,0:T(8,128)S(1)}, f32[352,128]{1,0:T(8,128)S(1)}, u32[]{:S(2)}, u32[]{:S(2)}) collective-permute-start(f32[352,128]{1,0:T(8,128)S(1)} %get-tuple-element.39), channel_id=1, source_target_pairs={{0,16},{32,48},{64,80},{96,112},{128,144},{160,176},{192,208},{224... | collective-permute-start | bytes 540680 | tf_op jit(solution)/shard_map/ppermute | solution.py:423
  26.0 19.3 %collective-permute-start.4 = (f32[352,128]{1,0:T(8,128)S(1)}, f32[352,128]{1,0:T(8,128)S(1)}, u32[]{:S(2)}, u32[]{:S(2)}) collective-permute-start(f32[352,128]{1,0:T(8,128)S(1)} %get-tuple-element.36), channel_id=1, source_target_pairs={{16,32},{48,64},{80,96},{112,128},{144,160},{176,192},{208,224},{0... | collective-permute-start | bytes 540680 | tf_op jit(solution)/shard_map/ppermute | solution.py:423
  32.6 12.7 %collective-permute-start.5 = (f32[352,128]{1,0:T(8,128)S(1)}, f32[352,128]{1,0:T(8,128)S(1)}, u32[]{:S(2)}, u32[]{:S(2)}) collective-permute-start(f32[352,128]{1,0:T(8,128)S(1)} %get-tuple-element.37), channel_id=1, source_target_pairs={{0,16},{32,48},{64,80},{96,112},{128,144},{160,176},{192,208},{224... | collective-permute-start | bytes 540680 | tf_op jit(solution)/shard_map/ppermute | solution.py:423
  39.9 5.4 %collective-permute-start.8 = (f32[8,32,128]{2,1,0:T(8,128)S(1)}, f32[8,32,128]{2,1,0:T(8,128)S(1)}, u32[]{:S(2)}, u32[]{:S(2)}) collective-permute-start(f32[8,32,128]{2,1,0:T(8,128)S(1)} %get-tuple-element.41), channel_id=1, source_target_pairs={{1,2},{3,4},{5,6},{7,8},{9,10},{11,12},{13,14},{0,64},{15,79},{17,... | collective-permute-start | bytes 393224 | tf_op jit(solution)/shard_map/ppermute | solution.py:423
  40.0 5.3 %collective-permute-start.9 = (f32[8,32,128]{2,1,0:T(8,128)S(1)}, f32[8,32,128]{2,1,0:T(8,128)S(1)}, u32[]{:S(2)}, u32[]{:S(2)}) collective-permute-start(f32[8,32,128]{2,1,0:T(8,128)S(1)} %get-tuple-element.42), channel_id=1, source_target_pairs={{0,1},{2,3},{4,5},{6,7},{8,9},{10,11},{12,13},{14,15},{16,17},{18,... | collective-permute-start | bytes 393224 | tf_op jit(solution)/shard_map/ppermute | solution.py:423
where the time goes:
time: 48.3 us; the launch traced here: 48.1 us
  starting transfers between devices  18.6 us (39%)
  waiting for transfers between devices  17.9 us (37%)
  Pallas kernels  9.77 us (20%)
  local copies, waits for them, and re-layouts  1.72 us (4%)
    ppermute x10, starting transfers between devices, swap(): lax.ppermute(cells, ('zg', 'xy'), pairing + [(j, i) for i, j in pairing])  18.6 us
    ppermute x10, waiting for transfers between devices, swap(): lax.ppermute(cells, ('zg', 'xy'), pairing + [(j, i) for i, j in pairing])  17.9 us
    pallas_call x6, Pallas kernels, call(): pl.pallas_call(kernel, out_shape=[shape(*dims) for dims in outs], in_spec...  9.77 us
    unnamed x7, local copies, waits for them, and re-layouts  1.72 us
  transfers between devices with their start and end apart: 10, of which 3 were waited for; matrix products, arithmetic and copies ran while one was open for 2% of the time, Pallas kernels for 5%

commit v1 on v0

--- a/solution.py
+++ b/solution.py
@@ -15,6 +15,7 @@
 LANES = 128
 CHUNKS = 8
 VMEM_LIMIT = 24 * 1024 * 1024
+PREPARE_LIMIT = 53 * 1024 * 1024
 
 
 SIDE = 4
@@ -24,7 +25,6 @@
 EDGE_PLANES = (0, 1, 2, 3, 8, 9, 10, 11)
 REST = 3 * SUB
 NEAR = HALF + REST
-CODES_AT = PLANES * NEAR
 RENEWED = (3, 3, 2, 1, 4, 4, 4, 4, 1, 2, 3, 3)
 RENEWED_AT = [SUB * sum(RENEWED[:plane]) for plane in range(PLANES + 1)]
 
@@ -165,35 +165,33 @@
     send(first, second, place, to_above, to_below, "zg")
 
 
-def prepare_kernel(
-    start_field, diffusivity, tile_block, block_material,
-    first, second, code,
-    own_v, own_d, own_t, material, tiles, field, conduct, to_first, to_second, codes, arrived, left,
-):
+def prepare_kernel(start_field, diffusivity, first, second, own_v, own_d, field, conduct, arrived):
     half = PLANES // 2
-    loads = [
-        pltpu.make_async_copy(tile_block, own_t, arrived.at[0]),
-        pltpu.make_async_copy(block_material, material, arrived.at[1]),
-    ]
-    for i, (source, target) in enumerate(((start_field, own_v), (diffusivity, own_d))):
-        for part in range(2):
-            at = pl.ds(part * half, half)
-            loads.append(
-                pltpu.make_async_copy(source.at[at], target.at[at], arrived.at[2 + 2 * i + part])
+    loads = []
+    for part in range(2):
+        at = pl.ds(part * half, half)
+        for source, target in ((start_field, own_v), (diffusivity, own_d)):
+            load = pltpu.make_async_copy(source.at[at], target.at[at], arrived.at[len(loads)])
+            load.start()
+            loads.append(load)
+    for part in range(2):
+        planes = range(part * half, part * half + half)
+        loads[2 * part].wait()
+        spread(own_v, field, 0, 0, planes)
+        loads[2 * part + 1].wait()
+        spread(own_d, conduct, 0, 0, planes)
+        for plane in planes:
+            at = plane * NEAR
+            send(first, second, pl.ds(at, HALF), field[plane, HALF:, :], field[plane, :HALF, :])
+            send(
+                first, second, pl.ds(at + HALF, REST),
+                conduct[plane, OWN_ROWS - REST :, :], conduct[plane, :REST, :],
             )
-    for load in loads:
-        load.start()
-    stores = []
-
-    def leave(source, target):
-        store = pltpu.make_async_copy(source, target, left.at[len(stores)])
-        store.start()
-        stores.append(store)
-
-    loads[0].wait()
-    loads[1].wait()
+
+
+def code_kernel(tile_block, material, first, second, code, tiles):
     tiles[...] = jnp.zeros(tiles.shape, jnp.int32)
-    tiles[:, :, : own_t.shape[2]] = own_t[...]
+    tiles[:, :, : tile_block.shape[2]] = tile_block[...]
     table = material[...]
     row = lax.broadcasted_iota(jnp.int32, (SUB, LANES), 0)
     bits = jnp.zeros((SUB, LANES), jnp.int32)
@@ -206,32 +204,10 @@
         entry = jnp.maximum(block - 1, 0)
         word = jnp.take_along_axis(bits, entry & (LANES - 1), axis=1)
         kind = (word >> (entry >> 7)) & 1
-        codes[plane] = jnp.where(block > 0, kind + 1, 0).astype(jnp.float32)
-        send(
-            to_first, to_second, pl.ds(CODES_AT + 3 * plane, 3),
-            codes[plane, 5:, :], codes[plane, :3, :],
-        )
-    for packet in (to_first, to_second):
-        packet[CODES_AT + 3 * PLANES :, :] = jnp.zeros((4, LANES), jnp.float32)
-    leave(codes, code)
-    for part in range(2):
-        planes = range(part * half, part * half + half)
-        loads[2 + part].wait()
-        spread(own_v, field, 0, 0, planes)
-        loads[4 + part].wait()
-        spread(own_d, conduct, 0, 0, planes)
-        for plane in planes:
-            at = plane * NEAR
-            send(to_first, to_second, pl.ds(at, HALF), field[plane, HALF:, :], field[plane, :HALF, :])
-            send(
-                to_first, to_second, pl.ds(at + HALF, REST),
-                conduct[plane, OWN_ROWS - REST :, :], conduct[plane, :REST, :],
-            )
-        at = pl.ds(0, half * NEAR) if part == 0 else pl.ds(half * NEAR, first.shape[0] - half * NEAR)
-        leave(to_first.at[at], first.at[at])
-        leave(to_second.at[at], second.at[at])
-    for store in stores:
-        store.wait()
+        code[plane] = jnp.where(block > 0, kind + 1, 0).astype(jnp.float32)
+        send(first, second, pl.ds(3 * plane, 3), code[plane, 5:, :], code[plane, :3, :])
+    for packet in (first, second):
+        packet[3 * PLANES :, :] = jnp.zeros((4, LANES), jnp.float32)
 
 
 def own_kernel(start_field, diffusivity, code, even, factor, marks, wide):
@@ -250,7 +226,7 @@
 
 
 def first_kernel(
-    near_first, near_second, field, conduct, code, couple,
+    near_first, near_second, code_first, code_second, field, conduct, code, couple,
     first, second, trace_first, trace_second, state, kept, factor, marks,
     even, odd, wide, codes,
 ):
@@ -269,7 +245,9 @@
             at = plane * NEAR
             even[plane + 1, pl.ds(near_at, HALF), :] = packet(at, HALF)
             factor[plane, pl.ds(rest_at, REST), :] = packet(at + HALF, REST)
-            codes[plane, place : place + 3, :] = packet(CODES_AT + 3 * plane, 3)
+            codes[plane, place : place + 3, :] = kept_if(
+                flag, got(code_first, code_second, pl.ds(3 * plane, 3), from_left)
+            )
         wide[...] = widened(codes[...])
         spread(wide, marks, offset, 0)
     even[1 : PLANES + 1, own, :] = field[:, own, :]
@@ -384,17 +362,18 @@
 CELLS = (PLANES, OWN_ROWS, LANES)
 TRACES = (TRACE_AT[-1], LANES)
 WIDE = (PLANES, OWN, CHUNKS * LANES)
-PACKET = (CODES_AT + 3 * PLANES + 4, LANES)
+PACKET = (PLANES * NEAR, LANES)
+CODES = (3 * PLANES + 4, LANES)
 SHARE = (RENEWED_AT[-1], LANES)
 EDGE_SHARE = (len(EDGE_PLANES), HALF, LANES)
 
 
-def call(kernel, outs, scratch, *operands, place=VMEM, out_place=VMEM, limit=VMEM_LIMIT):
+def call(kernel, outs, scratch, *operands, place=VMEM, limit=VMEM_LIMIT):
     return pl.pallas_call(
         kernel,
         out_shape=[shape(*dims) for dims in outs],
         in_specs=[place] * len(operands),
-        out_specs=[out_place] * len(outs),
+        out_specs=[VMEM] * len(outs),
         scratch_shapes=scratch,
         compiler_params=pltpu.CompilerParams(vmem_limit_bytes=limit),
         name=kernel.__name__,
@@ -432,23 +411,22 @@
         [jnp.block([[turned[kind], empty], [empty, turned[kind]]]) for kind in (0, 1)], axis=1
     )
     material = block_material.reshape(-1, LANES)
+    first, second = call(
+        prepare_kernel,
+        [PACKET, PACKET],
+        scratch(start_field.shape, diffusivity.shape, CELLS, CELLS) + [pltpu.SemaphoreType.DMA((4,))],
+        start_field, diffusivity,
+        place=HBM,
+        limit=PREPARE_LIMIT,
+    )
+    near = swap(first, second, "xy")
     first, second, code = call(
-        prepare_kernel,
-        [PACKET, PACKET, (PLANES, OWN, LANES)],
-        scratch(start_field.shape, diffusivity.shape)
-        + [
-            pltpu.VMEM(tile_block.shape, jnp.int32),
-            pltpu.VMEM(material.shape, jnp.int32),
-            pltpu.VMEM((PLANES, OWN, LANES), jnp.int32),
-        ]
-        + scratch(CELLS, CELLS, PACKET, PACKET, (PLANES, OWN, LANES))
-        + [pltpu.SemaphoreType.DMA((6,)), pltpu.SemaphoreType.DMA((5,))],
-        start_field, diffusivity, tile_block, material,
-        place=HBM,
-        out_place=HBM,
-        limit=56 * 1024 * 1024,
-    )
-    near = swap(first, second, "xy")
+        code_kernel,
+        [CODES, CODES, (PLANES, OWN, LANES)],
+        [pltpu.VMEM((PLANES, OWN, LANES), jnp.int32)],
+        tile_block, material,
+    )
+    codes = swap(first, second, "xy")
     field, conduct, code = call(
         own_kernel, [FIELD] * 3, scratch(WIDE), start_field, diffusivity, code
     )
@@ -456,7 +434,7 @@
         first_kernel,
         [SHARE, SHARE, TRACES, TRACES, CELLS, (len(EARLY_KEPT), ROWS * SUB, LANES), FIELD, FIELD],
         scratch(PADDED, PADDED, WIDE, (PLANES, OWN, LANES)),
-        *near, field, conduct, code, couple,
+        *near, *codes, field, conduct, code, couple,
     )
     sides = swap(first, second, "xy")
     early = swap(trace_first, trace_second, "zg")

time: 48.3 us -> 47.3 us (0.979)
  waiting for transfers between devices: 17.9 us -> 16.1 us
  Pallas kernels: 9.77 us -> 9.01 us
  local copies, waits for them, and re-layouts: 1.72 us -> 2.45 us
  starting transfers between devices: 18.6 us -> 19.3 us
    ppermute x10 -> x12, waiting for transfers between devices: 17.9 us -> 16.1 us  [swap(): lax.ppermute(cells, ('zg', 'xy'), pairing + [(j, i) for i, j in pairing])]
    pallas_call x6 -> x7, Pallas kernels: 9.77 us -> 9.01 us  [call(): pl.pallas_call(kernel, out_shape=[shape(*dims) for dims in outs], in_spec...]
    unnamed x7 -> x9, local copies, waits for them, and re-layouts: 1.72 us -> 2.44 us
    ppermute x10 -> x12, starting transfers between devices: 18.6 us -> 19.3 us  [swap(): lax.ppermute(cells, ('zg', 'xy'), pairing + [(j, i) for i, j in pairing])]
  transfers between devices with their start and end apart: 10 -> 12, of which waited for: 3 -> 3; matrix products, arithmetic and copies ran while one was open for 2% -> 2% of each run, Pallas kernels for 5% -> 5%
where the time goes in v1:
time: 47.3 us; the launch traced here: 47 us
  starting transfers between devices  19.3 us (41%)
  waiting for transfers between devices  16.1 us (34%)
  Pallas kernels  9.01 us (19%)
  local copies, waits for them, and re-layouts  2.45 us (5%)
    ppermute x12, starting transfers between devices, swap(): lax.ppermute(cells, ('zg', 'xy'), pairing + [(j, i) for i, j in pairing])  19.3 us
    ppermute x12, waiting for transfers between devices, swap(): lax.ppermute(cells, ('zg', 'xy'), pairing + [(j, i) for i, j in pairing])  16.1 us
    pallas_call x7, Pallas kernels, call(): pl.pallas_call(kernel, out_shape=[shape(*dims) for dims in outs], in_spec...  9.01 us
    unnamed x9, local copies, waits for them, and re-layouts  2.44 us
  transfers between devices with their start and end apart: 12, of which 3 were waited for; matrix products, arithmetic and copies ran while one was open for 2% of the time, Pallas kernels for 5%

profile of v1, /device:TPU:30, one launch (start us, length us, event | category | flops | bytes accessed | tf_op | source)
XLA Modules:
  0.0 47.0 jit_solution(13498538622896073071)
XLA Ops:
  0.0 1.4 %prepare_kernel.1 = (f32[672,128]{1,0:T(8,128)S(1)}, f32[672,128]{1,0:T(8,128)S(1)}) custom-call(f32[12,8,1024]{2,1,0:T(8,128)} %start_field.3, f32[12,8,1024]{2,1,0:T(8,128)} %diffusivity.3), custom_call_target="tpu_custom_call" | custom-call | tf_op jit(solution)/shard_map/prepare_kernel/pallas_call | solution.py:372
  1.4 1.7 %collective-permute-start = (f32[672,128]{1,0:T(8,128)S(1)}, f32[672,128]{1,0:T(8,128)S(1)}, u32[]{:S(2)}, u32[]{:S(2)}) collective-permute-start(f32[672,128]{1,0:T(8,128)S(1)} %get-tuple-element.27), channel_id=1, source_target_pairs={{1,2},{3,4},{5,6},{7,8},{9,10},{11,12},{13,14},{0,64},{15,79},{17,... | collective-permute-start | bytes 1032200 | tf_op jit(solution)/shard_map/ppermute | solution.py:402
  3.1 0.4 collective-permute-start.1
  3.5 0.8 %copy-done.2 = s32[12,8,16]{2,1,0:T(8,128)S(1)} copy-done((s32[12,8,16]{2,1,0:T(8,128)S(1)}, s32[12,8,16]{2,1,0:T(8,128)}, u32[]{:S(2)}) %copy-start.2) | copy-done | bytes 6168
  4.3 0.7 %copy-done.3 = s32[4096]{0:T(1024)S(1)} copy-done((s32[4096]{0:T(1024)S(1)}, s32[4096]{0:T(1024)}, u32[]{:S(2)}) %copy-start.3) | copy-done | bytes 16408
  5.0 0.1 code_kernel.1
  5.1 0.7 %collective-permute-start.2 = (f32[40,128]{1,0:T(8,128)S(1)}, f32[40,128]{1,0:T(8,128)S(1)}, u32[]{:S(2)}, u32[]{:S(2)}) collective-permute-start(f32[40,128]{1,0:T(8,128)S(1)} %get-tuple-element.29), channel_id=1, source_target_pairs={{1,2},{3,4},{5,6},{7,8},{9,10},{11,12},{13,14},{0,64},{15,79},{17,... | collective-permute-start | bytes 61448 | tf_op jit(solution)/shard_map/ppermute | solution.py:402
  5.9 0.9 %copy.6 = f32[2,64,64]{1,2,0:T(8,128)S(1)} copy(f32[2,64,64]{2,1,0:T(8,128)} %param.9) | data formatting | bytes 65536 | tf_op args[4]
  6.8 0.1 fusion.couple
  6.9 0.3 own_kernel.1
  7.2 5.8 %collective-permute-done.2.code_first = f32[40,128]{1,0:T(8,128)S(1)} collective-permute-done((f32[40,128]{1,0:T(8,128)S(1)}, f32[40,128]{1,0:T(8,128)S(1)}, u32[]{:S(2)}, u32[]{:S(2)}) %collective-permute-start.2) | collective-permute-done | bytes 20512 | tf_op jit(solution)/shard_map/ppermute | solution.py:402
  13.0 2.4 %first_kernel.1 = (f32[272,128]{1,0:T(8,128)S(1)}, f32[272,128]{1,0:T(8,128)S(1)}, f32[352,128]{1,0:T(8,128)S(1)}, f32[352,128]{1,0:T(8,128)S(1)}, f32[12,64,128...) custom-call(f32[672,128]{1,0:T(8,128)S(1)} %collective-permute-done.near, ...), custom_call_target="tpu_custom_call" | custom-call | tf_op jit(solution)/shard_map/first_kernel/pallas_call | solution.py:372
  15.4 1.6 %collective-permute-start.4 = (f32[272,128]{1,0:T(8,128)S(1)}, f32[272,128]{1,0:T(8,128)S(1)}, u32[]{:S(2)}, u32[]{:S(2)}) collective-permute-start(f32[272,128]{1,0:T(8,128)S(1)} %get-tuple-element.35), channel_id=1, source_target_pairs={{1,2},{3,4},{5,6},{7,8},{9,10},{11,12},{13,14},{0,64},{15,79},{17,... | collective-permute-start | bytes 417800 | tf_op jit(solution)/shard_map/ppermute | solution.py:402
  17.0 5.6 %collective-permute-start.8 = (f32[352,128]{1,0:T(8,128)S(1)}, f32[352,128]{1,0:T(8,128)S(1)}, u32[]{:S(2)}, u32[]{:S(2)}) collective-permute-start(f32[352,128]{1,0:T(8,128)S(1)} %get-tuple-element.42), channel_id=1, source_target_pairs={{16,32},{48,64},{80,96},{112,128},{144,160},{176,192},{208,224},{0... | collective-permute-start | bytes 540680 | tf_op jit(solution)/shard_map/ppermute | solution.py:402
  22.6 1.3 %collective-permute-start.9 = (f32[352,128]{1,0:T(8,128)S(1)}, f32[352,128]{1,0:T(8,128)S(1)}, u32[]{:S(2)}, u32[]{:S(2)}) collective-permute-start(f32[352,128]{1,0:T(8,128)S(1)} %get-tuple-element.43), channel_id=1, source_target_pairs={{0,16},{32,48},{64,80},{96,112},{128,144},{160,176},{192,208},{224... | collective-permute-start | bytes 540680 | tf_op jit(solution)/shard_map/ppermute | solution.py:402
  23.9 1.0 %middle_kernel.1 = (f32[352,128]{1,0:T(8,128)S(1)}, f32[352,128]{1,0:T(8,128)S(1)}, f32[6,192,128]{2,1,0:T(8,128)S(1)}) custom-call(f32[272,128]{1,0:T(8,128)S(1)} %collective-permute-done.4.first, f32[272,128]{1,0:T(8,128)S(1)} %collective-permute-done.5.second, f32[12,64,128]{2,1,0:T(8,128)S(1)} %get-tuple-element.37.state, ...), custom_call_target="tpu_custom_call" | custom-call | tf_op jit(solution)/shard_map/middle_kernel/pallas_call | solution.py:372
  24.9 6.6 %collective-permute-start.6 = (f32[352,128]{1,0:T(8,128)S(1)}, f32[352,128]{1,0:T(8,128)S(1)}, u32[]{:S(2)}, u32[]{:S(2)}) collective-permute-start(f32[352,128]{1,0:T(8,128)S(1)} %get-tuple-element.40), channel_id=1, source_target_pairs={{16,32},{48,64},{80,96},{112,128},{144,160},{176,192},{208,224},{0... | collective-permute-start | bytes 540680 | tf_op jit(solution)/shard_map/ppermute | solution.py:402
  31.5 1.2 %collective-permute-start.7 = (f32[352,128]{1,0:T(8,128)S(1)}, f32[352,128]{1,0:T(8,128)S(1)}, u32[]{:S(2)}, u32[]{:S(2)}) collective-permute-start(f32[352,128]{1,0:T(8,128)S(1)} %get-tuple-element.41), channel_id=1, source_target_pairs={{0,16},{32,48},{64,80},{96,112},{128,144},{160,176},{192,208},{224... | collective-permute-start | bytes 540680 | tf_op jit(solution)/shard_map/ppermute | solution.py:402
  32.7 5.1 %collective-permute-done.8.trace_first = f32[352,128]{1,0:T(8,128)S(1)} collective-permute-done((f32[352,128]{1,0:T(8,128)S(1)}, f32[352,128]{1,0:T(8,128)S(1)}, u32[]{:S(2)}, u32[]{:S(2)}) %collective-permute-start.8) | collective-permute-done | bytes 180256 | tf_op jit(solution)/shard_map/ppermute | solution.py:402
  37.8 1.0 %second_kernel.1 = (f32[8,32,128]{2,1,0:T(8,128)S(1)}, f32[8,32,128]{2,1,0:T(8,128)S(1)}, f32[8,64,128]{2,1,0:T(8,128)S(1)}) custom-call(f32[352,128]{1,0:T(8,128)S(1)} %collective-permute-done.8.trace_first, f32[352,128]{1,0:T(8,128)S(1)} %collective-permute-done.9.trace_second, f32[16,192,128]{2,1,0:T(8,128)S(1)} %get-tuple-element.44.kept, ...), custom_call_target="tpu_custom_call" | custom-call | tf_op jit(solution)/shard_map/second_kernel/pallas_call | solution.py:372
  38.8 0.1 collective-permute-start.10
  38.9 0.1 collective-permute-start.11
  39.0 5.2 %collective-permute-done.10.first = f32[8,32,128]{2,1,0:T(8,128)S(1)} collective-permute-done((f32[8,32,128]{2,1,0:T(8,128)S(1)}, f32[8,32,128]{2,1,0:T(8,128)S(1)}, u32[]{:S(2)}, u32[]{:S(2)}) %collective-permute-start.10) | collective-permute-done | bytes 131104 | tf_op jit(solution)/shard_map/ppermute | solution.py:402
  44.2 2.8 %last_kernel.1 = f32[12,8,1024]{2,1,0:T(8,128)} custom-call(f32[352,128]{1,0:T(8,128)S(1)} %collective-permute-done.6.trace_first, f32[352,128]{1,0:T(8,128)S(1)} %collective-permute-done.7.trace_second, f32[8,32,128]{2,1,0:T(8,128)S(1)} %collective-permute-done.10.first, f32[8,32,128]{2,1,0:T(8,128)S(1)} %collective-permute-done.11.second, ...), custom_call_target="tpu_custom_call" | custom-call | tf_op jit(solution)/shard_map/last_kernel/pallas_call | solution.py:372
  (18 shorter events, 0.0 us)
Async XLA Ops:
  0.0 6.9 %copy-start.1 = (f32[12,8,1024]{2,1,0:T(8,128)S(1)}, f32[12,8,1024]{2,1,0:T(8,128)}, u32[]{:S(2)}) copy-start(f32[12,8,1024]{2,1,0:T(8,128)} %diffusivity.3) | copy-start | bytes 1179652
  0.0 6.9 %copy-start = (f32[12,8,1024]{2,1,0:T(8,128)S(1)}, f32[12,8,1024]{2,1,0:T(8,128)}, u32[]{:S(2)}) copy-start(f32[12,8,1024]{2,1,0:T(8,128)} %start_field.3) | copy-start | bytes 1179652
  1.4 11.6 %collective-permute-start = (f32[672,128]{1,0:T(8,128)S(1)}, f32[672,128]{1,0:T(8,128)S(1)}, u32[]{:S(2)}, u32[]{:S(2)}) collective-permute-start(f32[672,128]{1,0:T(8,128)S(1)} %get-tuple-element.27), channel_id=1, source_target_pairs={{1,2},{3,4},{5,6},{7,8},{9,10},{11,12},{13,14},{0,64},{15,79},{17,... | collective-permute-start | bytes 1032200 | tf_op jit(solution)/shard_map/ppermute | solution.py:402
  3.1 9.9 %collective-permute-start.1 = (f32[672,128]{1,0:T(8,128)S(1)}, f32[672,128]{1,0:T(8,128)S(1)}, u32[]{:S(2)}, u32[]{:S(2)}) collective-permute-start(f32[672,128]{1,0:T(8,128)S(1)} %get-tuple-element.28), channel_id=1, source_target_pairs={{0,1},{2,3},{4,5},{6,7},{8,9},{10,11},{12,13},{14,15},{16,17},{18,... | collective-permute-start | bytes 1032200 | tf_op jit(solution)/shard_map/ppermute | solution.py:402
  3.5 0.8 %copy-start.2 = (s32[12,8,16]{2,1,0:T(8,128)S(1)}, s32[12,8,16]{2,1,0:T(8,128)}, u32[]{:S(2)}) copy-start(s32[12,8,16]{2,1,0:T(8,128)} %tile_block.1) | copy-start | bytes 18436
  4.3 0.7 %copy-start.3 = (s32[4096]{0:T(1024)S(1)}, s32[4096]{0:T(1024)}, u32[]{:S(2)}) copy-start(s32[4096]{0:T(1024)} %param.8) | copy-start | bytes 49156
  5.1 7.9 %collective-permute-start.2 = (f32[40,128]{1,0:T(8,128)S(1)}, f32[40,128]{1,0:T(8,128)S(1)}, u32[]{:S(2)}, u32[]{:S(2)}) collective-permute-start(f32[40,128]{1,0:T(8,128)S(1)} %get-tuple-element.29), channel_id=1, source_target_pairs={{1,2},{3,4},{5,6},{7,8},{9,10},{11,12},{13,14},{0,64},{15,79},{17,... | collective-permute-start | bytes 61448 | tf_op jit(solution)/shard_map/ppermute | solution.py:402
  5.8 7.2 %collective-permute-start.3 = (f32[40,128]{1,0:T(8,128)S(1)}, f32[40,128]{1,0:T(8,128)S(1)}, u32[]{:S(2)}, u32[]{:S(2)}) collective-permute-start(f32[40,128]{1,0:T(8,128)S(1)} %get-tuple-element.30), channel_id=1, source_target_pairs={{0,1},{2,3},{4,5},{6,7},{8,9},{10,11},{12,13},{14,15},{16,17},{18,... | collective-permute-start | bytes 61448 | tf_op jit(solution)/shard_map/ppermute | solution.py:402
  15.4 8.5 %collective-permute-start.4 = (f32[272,128]{1,0:T(8,128)S(1)}, f32[272,128]{1,0:T(8,128)S(1)}, u32[]{:S(2)}, u32[]{:S(2)}) collective-permute-start(f32[272,128]{1,0:T(8,128)S(1)} %get-tuple-element.35), channel_id=1, source_target_pairs={{1,2},{3,4},{5,6},{7,8},{9,10},{11,12},{13,14},{0,64},{15,79},{17,... | collective-permute-start | bytes 417800 | tf_op jit(solution)/shard_map/ppermute | solution.py:402
  17.0 6.9 %collective-permute-start.5 = (f32[272,128]{1,0:T(8,128)S(1)}, f32[272,128]{1,0:T(8,128)S(1)}, u32[]{:S(2)}, u32[]{:S(2)}) collective-permute-start(f32[272,128]{1,0:T(8,128)S(1)} %get-tuple-element.36), channel_id=1, source_target_pairs={{0,1},{2,3},{4,5},{6,7},{8,9},{10,11},{12,13},{14,15},{16,17},{18,... | collective-permute-start | bytes 417800 | tf_op jit(solution)/shard_map/ppermute | solution.py:402
  17.0 20.8 %collective-permute-start.8 = (f32[352,128]{1,0:T(8,128)S(1)}, f32[352,128]{1,0:T(8,128)S(1)}, u32[]{:S(2)}, u32[]{:S(2)}) collective-permute-start(f32[352,128]{1,0:T(8,128)S(1)} %get-tuple-element.42), channel_id=1, source_target_pairs={{16,32},{48,64},{80,96},{112,128},{144,160},{176,192},{208,224},{0... | collective-permute-start | bytes 540680 | tf_op jit(solution)/shard_map/ppermute | solution.py:402
  22.6 15.2 %collective-permute-start.9 = (f32[352,128]{1,0:T(8,128)S(1)}, f32[352,128]{1,0:T(8,128)S(1)}, u32[]{:S(2)}, u32[]{:S(2)}) collective-permute-start(f32[352,128]{1,0:T(8,128)S(1)} %get-tuple-element.43), channel_id=1, source_target_pairs={{0,16},{32,48},{64,80},{96,112},{128,144},{160,176},{192,208},{224... | collective-permute-start | bytes 540680 | tf_op jit(solution)/shard_map/ppermute | solution.py:402
  24.9 19.3 %collective-permute-start.6 = (f32[352,128]{1,0:T(8,128)S(1)}, f32[352,128]{1,0:T(8,128)S(1)}, u32[]{:S(2)}, u32[]{:S(2)}) collective-permute-start(f32[352,128]{1,0:T(8,128)S(1)} %get-tuple-element.40), channel_id=1, source_target_pairs={{16,32},{48,64},{80,96},{112,128},{144,160},{176,192},{208,224},{0... | collective-permute-start | bytes 540680 | tf_op jit(solution)/shard_map/ppermute | solution.py:402
  31.5 12.7 %collective-permute-start.7 = (f32[352,128]{1,0:T(8,128)S(1)}, f32[352,128]{1,0:T(8,128)S(1)}, u32[]{:S(2)}, u32[]{:S(2)}) collective-permute-start(f32[352,128]{1,0:T(8,128)S(1)} %get-tuple-element.41), channel_id=1, source_target_pairs={{0,16},{32,48},{64,80},{96,112},{128,144},{160,176},{192,208},{224... | collective-permute-start | bytes 540680 | tf_op jit(solution)/shard_map/ppermute | solution.py:402
  38.8 5.4 %collective-permute-start.10 = (f32[8,32,128]{2,1,0:T(8,128)S(1)}, f32[8,32,128]{2,1,0:T(8,128)S(1)}, u32[]{:S(2)}, u32[]{:S(2)}) collective-permute-start(f32[8,32,128]{2,1,0:T(8,128)S(1)} %get-tuple-element.45), channel_id=1, source_target_pairs={{1,2},{3,4},{5,6},{7,8},{9,10},{11,12},{13,14},{0,64},{15,79},{17,... | collective-permute-start | bytes 393224 | tf_op jit(solution)/shard_map/ppermute | solution.py:402
  38.9 5.3 %collective-permute-start.11 = (f32[8,32,128]{2,1,0:T(8,128)S(1)}, f32[8,32,128]{2,1,0:T(8,128)S(1)}, u32[]{:S(2)}, u32[]{:S(2)}) collective-permute-start(f32[8,32,128]{2,1,0:T(8,128)S(1)} %get-tuple-element.46), channel_id=1, source_target_pairs={{0,1},{2,3},{4,5},{6,7},{8,9},{10,11},{12,13},{14,15},{16,17},{18,... | collective-permute-start | bytes 393224 | tf_op jit(solution)/shard_map/ppermute | solution.py:402

commit v2 on v1

--- a/solution.py
+++ b/solution.py
@@ -210,11 +210,25 @@
         packet[3 * PLANES :, :] = jnp.zeros((4, LANES), jnp.float32)
 
 
-def own_kernel(start_field, diffusivity, code, even, factor, marks, wide):
-    spread(start_field, even, HALO, 0)
+def own_kernel(
+    start_field, diffusivity, code, couple,
+    field, factor, marks, inner_1, inner_2, inner_3,
+    even, odd, wide,
+):
+    own = pl.ds(OWN_AT, OWN_ROWS)
+    spread(start_field, even, HALO, 1)
     spread(diffusivity, factor, HALO, 0)
     wide[...] = widened(code[...])
     spread(wide, marks, HALO, 0)
+    field[...] = even[1 : PLANES + 1, own, :]
+    weight = weights(couple)
+    buffers = (even, odd)
+    for level, inner in enumerate((inner_1, inner_2, inner_3)):
+        src, dst = buffers[level % 2], buffers[1 - level % 2]
+        low, high = HALO + 1 + level, HALO + OWN - 1 - level
+        ghosts(src, low, high)
+        advance(src, dst, factor, marks, weight, 0, PLANES, low, high)
+        inner[...] = dst[1 : PLANES + 1, span(low, high), :]
 
 
 def keep(src, kept, places, level):
@@ -226,7 +240,8 @@
 
 
 def first_kernel(
-    near_first, near_second, code_first, code_second, field, conduct, code, couple,
+    near_first, near_second, code_first, code_second,
+    field, conduct, code, inner_1, inner_2, inner_3, couple,
     first, second, trace_first, trace_second, state, kept, factor, marks,
     even, odd, wide, codes,
 ):
@@ -250,7 +265,7 @@
             )
         wide[...] = widened(codes[...])
         spread(wide, marks, offset, 0)
-    even[1 : PLANES + 1, own, :] = field[:, own, :]
+    even[1 : PLANES + 1, own, :] = field[...]
     factor[:, own, :] = conduct[:, own, :]
     marks[:, own, :] = code[:, own, :]
     buffers = (even, odd)
@@ -260,7 +275,11 @@
         keep(src, kept, EARLY_KEPT, level)
         low, high = reach(level)
         ghosts(src, low, high)
-        advance_groups(src, dst, factor, marks, weight, 3, 4, 4, low, high)
+        for outer in (low, high - SIDE):
+            advance(src, dst, factor, marks, weight, 0, PLANES, outer, outer + SIDE)
+        if level < SIDE - 1:
+            inner = (inner_1, inner_2, inner_3)[level]
+            dst[1 : PLANES + 1, span(low + SIDE, high - SIDE), :] = inner[...]
     state[...] = even[1 : PLANES + 1, OWN_AT : OWN_AT + OWN_ROWS, :]
     for plane in range(PLANES):
         rows = RENEWED[plane] * SUB
@@ -427,14 +446,17 @@
         tile_block, material,
     )
     codes = swap(first, second, "xy")
-    field, conduct, code = call(
-        own_kernel, [FIELD] * 3, scratch(WIDE), start_field, diffusivity, code
+    field, conduct, code, *inner = call(
+        own_kernel,
+        [CELLS, FIELD, FIELD] + [(PLANES, (OWN - 2 * level) * SUB, LANES) for level in (1, 2, 3)],
+        scratch(PADDED, PADDED, WIDE),
+        start_field, diffusivity, code, couple,
     )
     first, second, trace_first, trace_second, state, early_kept, factor, marks = call(
         first_kernel,
         [SHARE, SHARE, TRACES, TRACES, CELLS, (len(EARLY_KEPT), ROWS * SUB, LANES), FIELD, FIELD],
         scratch(PADDED, PADDED, WIDE, (PLANES, OWN, LANES)),
-        *near, *codes, field, conduct, code, couple,
+        *near, *codes, field, conduct, code, *inner, couple,
     )
     sides = swap(first, second, "xy")
     early = swap(trace_first, trace_second, "zg")

time: 47.3 us -> 46.6 us (0.985)
  waiting for transfers between devices: 16.1 us -> 15.5 us
    ppermute x12, waiting for transfers between devices: 16.1 us -> 15.5 us  [swap(): lax.ppermute(cells, ('zg', 'xy'), pairing + [(j, i) for i, j in pairing])]
  transfers between devices with their start and end apart: 12 -> 12, of which waited for: 3 -> 3; matrix products, arithmetic and copies ran while one was open for 2% -> 2% of each run, Pallas kernels for 5% -> 7%
where the time goes in v2:
time: 46.6 us; the launch traced here: 46.3 us
  starting transfers between devices  19.3 us (41%)
  waiting for transfers between devices  15.5 us (33%)
  Pallas kernels  8.97 us (19%)
  local copies, waits for them, and re-layouts  2.45 us (5%)
    ppermute x12, starting transfers between devices, swap(): lax.ppermute(cells, ('zg', 'xy'), pairing + [(j, i) for i, j in pairing])  19.3 us
    ppermute x12, waiting for transfers between devices, swap(): lax.ppermute(cells, ('zg', 'xy'), pairing + [(j, i) for i, j in pairing])  15.5 us
    pallas_call x7, Pallas kernels, call(): pl.pallas_call(kernel, out_shape=[shape(*dims) for dims in outs], in_spec...  8.97 us
    unnamed x9, local copies, waits for them, and re-layouts  2.44 us
  transfers between devices with their start and end apart: 12, of which 3 were waited for; matrix products, arithmetic and copies ran while one was open for 2% of the time, Pallas kernels for 7%

profile of v2, /device:TPU:30, one launch (start us, length us, event | category | flops | bytes accessed | tf_op | source)
XLA Modules:
  0.0 46.3 jit_solution(18233421191160951928)
XLA Ops:
  0.0 1.4 %prepare_kernel.1 = (f32[672,128]{1,0:T(8,128)S(1)}, f32[672,128]{1,0:T(8,128)S(1)}) custom-call(f32[12,8,1024]{2,1,0:T(8,128)} %start_field.3, f32[12,8,1024]{2,1,0:T(8,128)} %diffusivity.3), custom_call_target="tpu_custom_call" | custom-call | tf_op jit(solution)/shard_map/prepare_kernel/pallas_call | solution.py:391
  1.4 1.7 %collective-permute-start = (f32[672,128]{1,0:T(8,128)S(1)}, f32[672,128]{1,0:T(8,128)S(1)}, u32[]{:S(2)}, u32[]{:S(2)}) collective-permute-start(f32[672,128]{1,0:T(8,128)S(1)} %get-tuple-element.30), channel_id=1, source_target_pairs={{1,2},{3,4},{5,6},{7,8},{9,10},{11,12},{13,14},{0,64},{15,79},{17,... | collective-permute-start | bytes 1032200 | tf_op jit(solution)/shard_map/ppermute | solution.py:421
  3.1 0.4 collective-permute-start.1
  3.5 0.8 %copy-done.2 = s32[12,8,16]{2,1,0:T(8,128)S(1)} copy-done((s32[12,8,16]{2,1,0:T(8,128)S(1)}, s32[12,8,16]{2,1,0:T(8,128)}, u32[]{:S(2)}) %copy-start.2) | copy-done | bytes 6168
  4.3 0.7 %copy-done.3 = s32[4096]{0:T(1024)S(1)} copy-done((s32[4096]{0:T(1024)S(1)}, s32[4096]{0:T(1024)}, u32[]{:S(2)}) %copy-start.3) | copy-done | bytes 16408
  5.0 0.1 code_kernel.1
  5.1 0.7 %collective-permute-start.2 = (f32[40,128]{1,0:T(8,128)S(1)}, f32[40,128]{1,0:T(8,128)S(1)}, u32[]{:S(2)}, u32[]{:S(2)}) collective-permute-start(f32[40,128]{1,0:T(8,128)S(1)} %get-tuple-element.32), channel_id=1, source_target_pairs={{1,2},{3,4},{5,6},{7,8},{9,10},{11,12},{13,14},{0,64},{15,79},{17,... | collective-permute-start | bytes 61448 | tf_op jit(solution)/shard_map/ppermute | solution.py:421
  5.9 0.9 %copy.6 = f32[2,64,64]{1,2,0:T(8,128)S(1)} copy(f32[2,64,64]{2,1,0:T(8,128)} %param.9) | data formatting | bytes 65536 | tf_op args[4]
  6.8 0.1 fusion.couple
  6.9 0.9 %own_kernel.1 = (f32[12,64,128]{2,1,0:T(8,128)S(1)}, f32[12,192,128]{2,1,0:T(8,128)S(1)}, f32[12,192,128]{2,1,0:T(8,128)S(1)}, f32[12,48,128]{2,1,0:T(8,128)S(1)...) custom-call(f32[12,8,1024]{2,1,0:T(8,128)S(1)} %copy-done, f32[12,8,1024]{2,1,0:T(8,128)S(1)} %copy-done.1, ...), custom_call_target="tpu_custom_call" | custom-call | tf_op jit(solution)/shard_map/own_kernel/pallas_call | solution.py:391
  7.8 5.2 %collective-permute-done.2.code_first = f32[40,128]{1,0:T(8,128)S(1)} collective-permute-done((f32[40,128]{1,0:T(8,128)S(1)}, f32[40,128]{1,0:T(8,128)S(1)}, u32[]{:S(2)}, u32[]{:S(2)}) %collective-permute-start.2) | collective-permute-done | bytes 20512 | tf_op jit(solution)/shard_map/ppermute | solution.py:421
  13.0 1.7 %first_kernel.1 = (f32[272,128]{1,0:T(8,128)S(1)}, f32[272,128]{1,0:T(8,128)S(1)}, f32[352,128]{1,0:T(8,128)S(1)}, f32[352,128]{1,0:T(8,128)S(1)}, f32[12,64,128...) custom-call(f32[672,128]{1,0:T(8,128)S(1)} %collective-permute-done.near, ...), custom_call_target="tpu_custom_call" | custom-call | tf_op jit(solution)/shard_map/first_kernel/pallas_call | solution.py:391
  14.8 1.6 %collective-permute-start.4 = (f32[272,128]{1,0:T(8,128)S(1)}, f32[272,128]{1,0:T(8,128)S(1)}, u32[]{:S(2)}, u32[]{:S(2)}) collective-permute-start(f32[272,128]{1,0:T(8,128)S(1)} %get-tuple-element.41), channel_id=1, source_target_pairs={{1,2},{3,4},{5,6},{7,8},{9,10},{11,12},{13,14},{0,64},{15,79},{17,... | collective-permute-start | bytes 417800 | tf_op jit(solution)/shard_map/ppermute | solution.py:421
  16.4 5.6 %collective-permute-start.8 = (f32[352,128]{1,0:T(8,128)S(1)}, f32[352,128]{1,0:T(8,128)S(1)}, u32[]{:S(2)}, u32[]{:S(2)}) collective-permute-start(f32[352,128]{1,0:T(8,128)S(1)} %get-tuple-element.48), channel_id=1, source_target_pairs={{16,32},{48,64},{80,96},{112,128},{144,160},{176,192},{208,224},{0... | collective-permute-start | bytes 540680 | tf_op jit(solution)/shard_map/ppermute | solution.py:421
  21.9 1.3 %collective-permute-start.9 = (f32[352,128]{1,0:T(8,128)S(1)}, f32[352,128]{1,0:T(8,128)S(1)}, u32[]{:S(2)}, u32[]{:S(2)}) collective-permute-start(f32[352,128]{1,0:T(8,128)S(1)} %get-tuple-element.49), channel_id=1, source_target_pairs={{0,16},{32,48},{64,80},{96,112},{128,144},{160,176},{192,208},{224... | collective-permute-start | bytes 540680 | tf_op jit(solution)/shard_map/ppermute | solution.py:421
  23.2 1.0 %middle_kernel.1 = (f32[352,128]{1,0:T(8,128)S(1)}, f32[352,128]{1,0:T(8,128)S(1)}, f32[6,192,128]{2,1,0:T(8,128)S(1)}) custom-call(f32[272,128]{1,0:T(8,128)S(1)} %collective-permute-done.4.first, f32[272,128]{1,0:T(8,128)S(1)} %collective-permute-done.5.second, f32[12,64,128]{2,1,0:T(8,128)S(1)} %get-tuple-element.43.state, ...), custom_call_target="tpu_custom_call" | custom-call | tf_op jit(solution)/shard_map/middle_kernel/pallas_call | solution.py:391
  24.2 6.6 %collective-permute-start.6 = (f32[352,128]{1,0:T(8,128)S(1)}, f32[352,128]{1,0:T(8,128)S(1)}, u32[]{:S(2)}, u32[]{:S(2)}) collective-permute-start(f32[352,128]{1,0:T(8,128)S(1)} %get-tuple-element.46), channel_id=1, source_target_pairs={{16,32},{48,64},{80,96},{112,128},{144,160},{176,192},{208,224},{0... | collective-permute-start | bytes 540680 | tf_op jit(solution)/shard_map/ppermute | solution.py:421
  30.9 1.2 %collective-permute-start.7 = (f32[352,128]{1,0:T(8,128)S(1)}, f32[352,128]{1,0:T(8,128)S(1)}, u32[]{:S(2)}, u32[]{:S(2)}) collective-permute-start(f32[352,128]{1,0:T(8,128)S(1)} %get-tuple-element.47), channel_id=1, source_target_pairs={{0,16},{32,48},{64,80},{96,112},{128,144},{160,176},{192,208},{224... | collective-permute-start | bytes 540680 | tf_op jit(solution)/shard_map/ppermute | solution.py:421
  32.0 5.1 %collective-permute-done.8.trace_first = f32[352,128]{1,0:T(8,128)S(1)} collective-permute-done((f32[352,128]{1,0:T(8,128)S(1)}, f32[352,128]{1,0:T(8,128)S(1)}, u32[]{:S(2)}, u32[]{:S(2)}) %collective-permute-start.8) | collective-permute-done | bytes 180256 | tf_op jit(solution)/shard_map/ppermute | solution.py:421
  37.1 1.0 %second_kernel.1 = (f32[8,32,128]{2,1,0:T(8,128)S(1)}, f32[8,32,128]{2,1,0:T(8,128)S(1)}, f32[8,64,128]{2,1,0:T(8,128)S(1)}) custom-call(f32[352,128]{1,0:T(8,128)S(1)} %collective-permute-done.8.trace_first, f32[352,128]{1,0:T(8,128)S(1)} %collective-permute-done.9.trace_second, f32[16,192,128]{2,1,0:T(8,128)S(1)} %get-tuple-element.50.kept, ...), custom_call_target="tpu_custom_call" | custom-call | tf_op jit(solution)/shard_map/second_kernel/pallas_call | solution.py:391
  38.1 0.1 collective-permute-start.10
  38.2 0.1 collective-permute-start.11
  38.3 5.2 %collective-permute-done.10.first = f32[8,32,128]{2,1,0:T(8,128)S(1)} collective-permute-done((f32[8,32,128]{2,1,0:T(8,128)S(1)}, f32[8,32,128]{2,1,0:T(8,128)S(1)}, u32[]{:S(2)}, u32[]{:S(2)}) %collective-permute-start.10) | collective-permute-done | bytes 131104 | tf_op jit(solution)/shard_map/ppermute | solution.py:421
  43.5 2.8 %last_kernel.1 = f32[12,8,1024]{2,1,0:T(8,128)} custom-call(f32[352,128]{1,0:T(8,128)S(1)} %collective-permute-done.6.trace_first, f32[352,128]{1,0:T(8,128)S(1)} %collective-permute-done.7.trace_second, f32[8,32,128]{2,1,0:T(8,128)S(1)} %collective-permute-done.10.first, f32[8,32,128]{2,1,0:T(8,128)S(1)} %collective-permute-done.11.second, ...), custom_call_target="tpu_custom_call" | custom-call | tf_op jit(solution)/shard_map/last_kernel/pallas_call | solution.py:391
  (18 shorter events, 0.0 us)
Async XLA Ops:
  0.0 6.9 %copy-start.1 = (f32[12,8,1024]{2,1,0:T(8,128)S(1)}, f32[12,8,1024]{2,1,0:T(8,128)}, u32[]{:S(2)}) copy-start(f32[12,8,1024]{2,1,0:T(8,128)} %diffusivity.3) | copy-start | bytes 1179652
  0.0 6.9 %copy-start = (f32[12,8,1024]{2,1,0:T(8,128)S(1)}, f32[12,8,1024]{2,1,0:T(8,128)}, u32[]{:S(2)}) copy-start(f32[12,8,1024]{2,1,0:T(8,128)} %start_field.3) | copy-start | bytes 1179652
  1.4 11.6 %collective-permute-start = (f32[672,128]{1,0:T(8,128)S(1)}, f32[672,128]{1,0:T(8,128)S(1)}, u32[]{:S(2)}, u32[]{:S(2)}) collective-permute-start(f32[672,128]{1,0:T(8,128)S(1)} %get-tuple-element.30), channel_id=1, source_target_pairs={{1,2},{3,4},{5,6},{7,8},{9,10},{11,12},{13,14},{0,64},{15,79},{17,... | collective-permute-start | bytes 1032200 | tf_op jit(solution)/shard_map/ppermute | solution.py:421
  3.1 9.9 %collective-permute-start.1 = (f32[672,128]{1,0:T(8,128)S(1)}, f32[672,128]{1,0:T(8,128)S(1)}, u32[]{:S(2)}, u32[]{:S(2)}) collective-permute-start(f32[672,128]{1,0:T(8,128)S(1)} %get-tuple-element.31), channel_id=1, source_target_pairs={{0,1},{2,3},{4,5},{6,7},{8,9},{10,11},{12,13},{14,15},{16,17},{18,... | collective-permute-start | bytes 1032200 | tf_op jit(solution)/shard_map/ppermute | solution.py:421
  3.5 0.8 %copy-start.2 = (s32[12,8,16]{2,1,0:T(8,128)S(1)}, s32[12,8,16]{2,1,0:T(8,128)}, u32[]{:S(2)}) copy-start(s32[12,8,16]{2,1,0:T(8,128)} %tile_block.1) | copy-start | bytes 18436
  4.3 0.7 %copy-start.3 = (s32[4096]{0:T(1024)S(1)}, s32[4096]{0:T(1024)}, u32[]{:S(2)}) copy-start(s32[4096]{0:T(1024)} %param.8) | copy-start | bytes 49156
  5.1 7.9 %collective-permute-start.2 = (f32[40,128]{1,0:T(8,128)S(1)}, f32[40,128]{1,0:T(8,128)S(1)}, u32[]{:S(2)}, u32[]{:S(2)}) collective-permute-start(f32[40,128]{1,0:T(8,128)S(1)} %get-tuple-element.32), channel_id=1, source_target_pairs={{1,2},{3,4},{5,6},{7,8},{9,10},{11,12},{13,14},{0,64},{15,79},{17,... | collective-permute-start | bytes 61448 | tf_op jit(solution)/shard_map/ppermute | solution.py:421
  5.8 7.2 %collective-permute-start.3 = (f32[40,128]{1,0:T(8,128)S(1)}, f32[40,128]{1,0:T(8,128)S(1)}, u32[]{:S(2)}, u32[]{:S(2)}) collective-permute-start(f32[40,128]{1,0:T(8,128)S(1)} %get-tuple-element.33), channel_id=1, source_target_pairs={{0,1},{2,3},{4,5},{6,7},{8,9},{10,11},{12,13},{14,15},{16,17},{18,... | collective-permute-start | bytes 61448 | tf_op jit(solution)/shard_map/ppermute | solution.py:421
  14.8 8.5 %collective-permute-start.4 = (f32[272,128]{1,0:T(8,128)S(1)}, f32[272,128]{1,0:T(8,128)S(1)}, u32[]{:S(2)}, u32[]{:S(2)}) collective-permute-start(f32[272,128]{1,0:T(8,128)S(1)} %get-tuple-element.41), channel_id=1, source_target_pairs={{1,2},{3,4},{5,6},{7,8},{9,10},{11,12},{13,14},{0,64},{15,79},{17,... | collective-permute-start | bytes 417800 | tf_op jit(solution)/shard_map/ppermute | solution.py:421
  16.4 6.9 %collective-permute-start.5 = (f32[272,128]{1,0:T(8,128)S(1)}, f32[272,128]{1,0:T(8,128)S(1)}, u32[]{:S(2)}, u32[]{:S(2)}) collective-permute-start(f32[272,128]{1,0:T(8,128)S(1)} %get-tuple-element.42), channel_id=1, source_target_pairs={{0,1},{2,3},{4,5},{6,7},{8,9},{10,11},{12,13},{14,15},{16,17},{18,... | collective-permute-start | bytes 417800 | tf_op jit(solution)/shard_map/ppermute | solution.py:421
  16.4 20.8 %collective-permute-start.8 = (f32[352,128]{1,0:T(8,128)S(1)}, f32[352,128]{1,0:T(8,128)S(1)}, u32[]{:S(2)}, u32[]{:S(2)}) collective-permute-start(f32[352,128]{1,0:T(8,128)S(1)} %get-tuple-element.48), channel_id=1, source_target_pairs={{16,32},{48,64},{80,96},{112,128},{144,160},{176,192},{208,224},{0... | collective-permute-start | bytes 540680 | tf_op jit(solution)/shard_map/ppermute | solution.py:421
  21.9 15.2 %collective-permute-start.9 = (f32[352,128]{1,0:T(8,128)S(1)}, f32[352,128]{1,0:T(8,128)S(1)}, u32[]{:S(2)}, u32[]{:S(2)}) collective-permute-start(f32[352,128]{1,0:T(8,128)S(1)} %get-tuple-element.49), channel_id=1, source_target_pairs={{0,16},{32,48},{64,80},{96,112},{128,144},{160,176},{192,208},{224... | collective-permute-start | bytes 540680 | tf_op jit(solution)/shard_map/ppermute | solution.py:421
  24.2 19.3 %collective-permute-start.6 = (f32[352,128]{1,0:T(8,128)S(1)}, f32[352,128]{1,0:T(8,128)S(1)}, u32[]{:S(2)}, u32[]{:S(2)}) collective-permute-start(f32[352,128]{1,0:T(8,128)S(1)} %get-tuple-element.46), channel_id=1, source_target_pairs={{16,32},{48,64},{80,96},{112,128},{144,160},{176,192},{208,224},{0... | collective-permute-start | bytes 540680 | tf_op jit(solution)/shard_map/ppermute | solution.py:421
  30.9 12.7 %collective-permute-start.7 = (f32[352,128]{1,0:T(8,128)S(1)}, f32[352,128]{1,0:T(8,128)S(1)}, u32[]{:S(2)}, u32[]{:S(2)}) collective-permute-start(f32[352,128]{1,0:T(8,128)S(1)} %get-tuple-element.47), channel_id=1, source_target_pairs={{0,16},{32,48},{64,80},{96,112},{128,144},{160,176},{192,208},{224... | collective-permute-start | bytes 540680 | tf_op jit(solution)/shard_map/ppermute | solution.py:421
  38.1 5.4 %collective-permute-start.10 = (f32[8,32,128]{2,1,0:T(8,128)S(1)}, f32[8,32,128]{2,1,0:T(8,128)S(1)}, u32[]{:S(2)}, u32[]{:S(2)}) collective-permute-start(f32[8,32,128]{2,1,0:T(8,128)S(1)} %get-tuple-element.51), channel_id=1, source_target_pairs={{1,2},{3,4},{5,6},{7,8},{9,10},{11,12},{13,14},{0,64},{15,79},{17,... | collective-permute-start | bytes 393224 | tf_op jit(solution)/shard_map/ppermute | solution.py:421
  38.2 5.3 %collective-permute-start.11 = (f32[8,32,128]{2,1,0:T(8,128)S(1)}, f32[8,32,128]{2,1,0:T(8,128)S(1)}, u32[]{:S(2)}, u32[]{:S(2)}) collective-permute-start(f32[8,32,128]{2,1,0:T(8,128)S(1)} %get-tuple-element.52), channel_id=1, source_target_pairs={{0,1},{2,3},{4,5},{6,7},{8,9},{10,11},{12,13},{14,15},{16,17},{18,... | collective-permute-start | bytes 393224 | tf_op jit(solution)/shard_map/ppermute | solution.py:421

commit v3 on v2

--- a/solution.py
+++ b/solution.py
@@ -289,8 +289,23 @@
         )
 
 
+def inner_kernel(state, factor, marks, couple, inner_1, inner_2, inner_3, even, odd):
+    weight = weights(couple)
+    even[1 : PLANES + 1, pl.ds(OWN_AT, OWN_ROWS), :] = state[...]
+    buffers = (even, odd)
+    for step, inner in enumerate((inner_1, inner_2, inner_3)):
+        src, dst = buffers[step % 2], buffers[1 - step % 2]
+        low, high = HALO + 1 + step, HALO + OWN - 1 - step
+        ghosts(src, low, high)
+        groups, count, stride = ((3, 4, 4), (2, 3, 9), (2, 2, 10))[step]
+        advance_groups(src, dst, factor, marks, weight, groups, count, stride, low, high)
+        for i in range(groups):
+            plane = i * stride
+            inner[plane : plane + count] = dst[plane + 1 : plane + 1 + count, span(low, high), :]
+
+
 def middle_kernel(
-    first, second, state, factor, marks, couple,
+    first, second, state, inner_1, inner_2, inner_3, factor, marks, couple,
     trace_first, trace_second, kept,
     even, odd,
 ):
@@ -314,9 +329,16 @@
         low, high = reach(level)
         ghosts(src, low + 1, high - 1)
         count = STEPS - level
-        advance_groups(src, dst, factor, marks, weight, 2, count, PLANES - count, low + 1, high - 1)
+        inner = (inner_1, inner_2, inner_3)[level - SIDE]
+        for outer in (low + 1, high - SIDE):
+            advance_groups(src, dst, factor, marks, weight, 2, count, PLANES - count, outer, outer + 3)
+        parts = [(0, count), (PLANES - count, count)]
         if level == SIDE:
-            advance(src, dst, factor, marks, weight, 5, 2, low, high)
+            for outer in (low, high - SIDE):
+                advance(src, dst, factor, marks, weight, 5, 2, outer, outer + SIDE)
+            parts.append((5, 2))
+        for plane, size in parts:
+            dst[plane + 1 : plane + 1 + size, span(low + SIDE, high - SIDE), :] = inner[plane : plane + size]
 
 
 def second_steps(levels, buffers, kept, places, trace_first, trace_second, factor, marks, weight):
@@ -460,11 +482,17 @@
     )
     sides = swap(first, second, "xy")
     early = swap(trace_first, trace_second, "zg")
+    inner = call(
+        inner_kernel,
+        [(PLANES, (OWN - 2 * step) * SUB, LANES) for step in (1, 2, 3)],
+        scratch(PADDED, PADDED),
+        state, factor, marks, couple,
+    )
     trace_first, trace_second, late_kept = call(
         middle_kernel,
         [TRACES, TRACES, (len(LATE_KEPT), ROWS * SUB, LANES)],
         scratch(PADDED, PADDED),
-        *sides, state, factor, marks, couple,
+        *sides, state, *inner, factor, marks, couple,
     )
     late = swap(trace_first, trace_second, "zg")
     first, second, state = call(

time: 46.6 us -> 46.7 us (level)
  waiting for transfers between devices: 15.5 us -> 14.5 us
    ppermute x12, waiting for transfers between devices: 15.5 us -> 14.5 us  [swap(): lax.ppermute(cells, ('zg', 'xy'), pairing + [(j, i) for i, j in pairing])]
    pallas_call x7 -> x8, Pallas kernels: 8.97 us -> 9.37 us  [call(): pl.pallas_call(kernel, out_shape=[shape(*dims) for dims in outs], in_spec...]
where the time goes in v3:
time: 46.7 us; the launch traced here: 46.1 us
  starting transfers between devices  19.6 us (42%)
  waiting for transfers between devices  14.5 us (31%)
  Pallas kernels  9.37 us (20%)
  local copies, waits for them, and re-layouts  2.45 us (5%)
    ppermute x12, starting transfers between devices, swap(): lax.ppermute(cells, ('zg', 'xy'), pairing + [(j, i) for i, j in pairing])  19.6 us
    ppermute x12, waiting for transfers between devices, swap(): lax.ppermute(cells, ('zg', 'xy'), pairing + [(j, i) for i, j in pairing])  14.5 us
    pallas_call x8, Pallas kernels, call(): pl.pallas_call(kernel, out_shape=[shape(*dims) for dims in outs], in_spec...  9.37 us
    unnamed x9, local copies, waits for them, and re-layouts  2.44 us
  transfers between devices with their start and end apart: 12, of which 3 were waited for; matrix products, arithmetic and copies ran while one was open for 2% of the time, Pallas kernels for 7%

profile of v3, /device:TPU:30, one launch (start us, length us, event | category | flops | bytes accessed | tf_op | source)
XLA Modules:
  0.0 46.1 jit_solution(15809156574869674686)
XLA Ops:
  0.0 1.4 %prepare_kernel.1 = (f32[672,128]{1,0:T(8,128)S(1)}, f32[672,128]{1,0:T(8,128)S(1)}) custom-call(f32[12,8,1024]{2,1,0:T(8,128)} %start_field.3, f32[12,8,1024]{2,1,0:T(8,128)} %diffusivity.3), custom_call_target="tpu_custom_call" | custom-call | tf_op jit(solution)/shard_map/prepare_kernel/pallas_call | solution.py:413
  1.4 1.7 %collective-permute-start = (f32[672,128]{1,0:T(8,128)S(1)}, f32[672,128]{1,0:T(8,128)S(1)}, u32[]{:S(2)}, u32[]{:S(2)}) collective-permute-start(f32[672,128]{1,0:T(8,128)S(1)} %get-tuple-element.33), channel_id=1, source_target_pairs={{1,2},{3,4},{5,6},{7,8},{9,10},{11,12},{13,14},{0,64},{15,79},{17,... | collective-permute-start | bytes 1032200 | tf_op jit(solution)/shard_map/ppermute | solution.py:443
  3.1 0.4 collective-permute-start.1
  3.5 0.8 %copy-done.2 = s32[12,8,16]{2,1,0:T(8,128)S(1)} copy-done((s32[12,8,16]{2,1,0:T(8,128)S(1)}, s32[12,8,16]{2,1,0:T(8,128)}, u32[]{:S(2)}) %copy-start.2) | copy-done | bytes 6168
  4.3 0.7 %copy-done.3 = s32[4096]{0:T(1024)S(1)} copy-done((s32[4096]{0:T(1024)S(1)}, s32[4096]{0:T(1024)}, u32[]{:S(2)}) %copy-start.3) | copy-done | bytes 16408
  5.0 0.1 code_kernel.1
  5.1 0.7 %collective-permute-start.2 = (f32[40,128]{1,0:T(8,128)S(1)}, f32[40,128]{1,0:T(8,128)S(1)}, u32[]{:S(2)}, u32[]{:S(2)}) collective-permute-start(f32[40,128]{1,0:T(8,128)S(1)} %get-tuple-element.35), channel_id=1, source_target_pairs={{1,2},{3,4},{5,6},{7,8},{9,10},{11,12},{13,14},{0,64},{15,79},{17,... | collective-permute-start | bytes 61448 | tf_op jit(solution)/shard_map/ppermute | solution.py:443
  5.9 0.9 %copy.6 = f32[2,64,64]{1,2,0:T(8,128)S(1)} copy(f32[2,64,64]{2,1,0:T(8,128)} %param.9) | data formatting | bytes 65536 | tf_op args[4]
  6.9 0.9 %own_kernel.1 = (f32[12,64,128]{2,1,0:T(8,128)S(1)}, f32[12,192,128]{2,1,0:T(8,128)S(1)}, f32[12,192,128]{2,1,0:T(8,128)S(1)}, f32[12,48,128]{2,1,0:T(8,128)S(1)...) custom-call(f32[12,8,1024]{2,1,0:T(8,128)S(1)} %copy-done, f32[12,8,1024]{2,1,0:T(8,128)S(1)} %copy-done.1, ...), custom_call_target="tpu_custom_call" | custom-call | tf_op jit(solution)/shard_map/own_kernel/pallas_call | solution.py:413
  7.8 5.2 %collective-permute-done.2.code_first = f32[40,128]{1,0:T(8,128)S(1)} collective-permute-done((f32[40,128]{1,0:T(8,128)S(1)}, f32[40,128]{1,0:T(8,128)S(1)}, u32[]{:S(2)}, u32[]{:S(2)}) %collective-permute-start.2) | collective-permute-done | bytes 20512 | tf_op jit(solution)/shard_map/ppermute | solution.py:443
  13.0 1.7 %first_kernel.1 = (f32[272,128]{1,0:T(8,128)S(1)}, f32[272,128]{1,0:T(8,128)S(1)}, f32[352,128]{1,0:T(8,128)S(1)}, f32[352,128]{1,0:T(8,128)S(1)}, f32[12,64,128...) custom-call(f32[672,128]{1,0:T(8,128)S(1)} %collective-permute-done.near, ...), custom_call_target="tpu_custom_call" | custom-call | tf_op jit(solution)/shard_map/first_kernel/pallas_call | solution.py:413
  14.8 1.6 %collective-permute-start.4 = (f32[272,128]{1,0:T(8,128)S(1)}, f32[272,128]{1,0:T(8,128)S(1)}, u32[]{:S(2)}, u32[]{:S(2)}) collective-permute-start(f32[272,128]{1,0:T(8,128)S(1)} %get-tuple-element.44), channel_id=1, source_target_pairs={{1,2},{3,4},{5,6},{7,8},{9,10},{11,12},{13,14},{0,64},{15,79},{17,... | collective-permute-start | bytes 417800 | tf_op jit(solution)/shard_map/ppermute | solution.py:443
  16.4 5.6 %collective-permute-start.8 = (f32[352,128]{1,0:T(8,128)S(1)}, f32[352,128]{1,0:T(8,128)S(1)}, u32[]{:S(2)}, u32[]{:S(2)}) collective-permute-start(f32[352,128]{1,0:T(8,128)S(1)} %get-tuple-element.54), channel_id=1, source_target_pairs={{16,32},{48,64},{80,96},{112,128},{144,160},{176,192},{208,224},{0... | collective-permute-start | bytes 540680 | tf_op jit(solution)/shard_map/ppermute | solution.py:443
  21.9 1.3 %collective-permute-start.9 = (f32[352,128]{1,0:T(8,128)S(1)}, f32[352,128]{1,0:T(8,128)S(1)}, u32[]{:S(2)}, u32[]{:S(2)}) collective-permute-start(f32[352,128]{1,0:T(8,128)S(1)} %get-tuple-element.55), channel_id=1, source_target_pairs={{0,16},{32,48},{64,80},{96,112},{128,144},{160,176},{192,208},{224... | collective-permute-start | bytes 540680 | tf_op jit(solution)/shard_map/ppermute | solution.py:443
  23.2 0.7 %inner_kernel.1 = (f32[12,48,128]{2,1,0:T(8,128)S(1)}, f32[12,32,128]{2,1,0:T(8,128)S(1)}, f32[12,16,128]{2,1,0:T(8,128)S(1)}) custom-call(f32[12,64,128]{2,1,0:T(8,128)S(1)} %get-tuple-element.46.state, f32[12,192,128]{2,1,0:T(8,128)S(1)} %get-tuple-element.47.factor, f32[12,192,128]{2,1,0:T(8,128)S(1)} %get-tuple-element.48.marks, f32[128,256]{1,0:T(8,128)S(1)} %fusion.couple), custom_call_target="tpu_custom_call" | custom-call | tf_op jit(solution)/shard_map/inner_kernel/pallas_call | solution.py:413
  23.9 0.7 %middle_kernel.1 = (f32[352,128]{1,0:T(8,128)S(1)}, f32[352,128]{1,0:T(8,128)S(1)}, f32[6,192,128]{2,1,0:T(8,128)S(1)}) custom-call(f32[272,128]{1,0:T(8,128)S(1)} %collective-permute-done.4.first, f32[272,128]{1,0:T(8,128)S(1)} %collective-permute-done.5.second, f32[12,64,128]{2,1,0:T(8,128)S(1)} %get-tuple-element.46.state, ...), custom_call_target="tpu_custom_call" | custom-call | tf_op jit(solution)/shard_map/middle_kernel/pallas_call | solution.py:413
  24.6 6.1 %collective-permute-start.6 = (f32[352,128]{1,0:T(8,128)S(1)}, f32[352,128]{1,0:T(8,128)S(1)}, u32[]{:S(2)}, u32[]{:S(2)}) collective-permute-start(f32[352,128]{1,0:T(8,128)S(1)} %get-tuple-element.52), channel_id=1, source_target_pairs={{16,32},{48,64},{80,96},{112,128},{144,160},{176,192},{208,224},{0... | collective-permute-start | bytes 540680 | tf_op jit(solution)/shard_map/ppermute | solution.py:443
  30.7 1.1 %collective-permute-start.7 = (f32[352,128]{1,0:T(8,128)S(1)}, f32[352,128]{1,0:T(8,128)S(1)}, u32[]{:S(2)}, u32[]{:S(2)}) collective-permute-start(f32[352,128]{1,0:T(8,128)S(1)} %get-tuple-element.53), channel_id=1, source_target_pairs={{0,16},{32,48},{64,80},{96,112},{128,144},{160,176},{192,208},{224... | collective-permute-start | bytes 540680 | tf_op jit(solution)/shard_map/ppermute | solution.py:443
  31.8 4.3 %collective-permute-done.8.trace_first = f32[352,128]{1,0:T(8,128)S(1)} collective-permute-done((f32[352,128]{1,0:T(8,128)S(1)}, f32[352,128]{1,0:T(8,128)S(1)}, u32[]{:S(2)}, u32[]{:S(2)}) %collective-permute-start.8) | collective-permute-done | bytes 180256 | tf_op jit(solution)/shard_map/ppermute | solution.py:443
  36.1 1.0 %second_kernel.1 = (f32[8,32,128]{2,1,0:T(8,128)S(1)}, f32[8,32,128]{2,1,0:T(8,128)S(1)}, f32[8,64,128]{2,1,0:T(8,128)S(1)}) custom-call(f32[352,128]{1,0:T(8,128)S(1)} %collective-permute-done.8.trace_first, f32[352,128]{1,0:T(8,128)S(1)} %collective-permute-done.9.trace_second, f32[16,192,128]{2,1,0:T(8,128)S(1)} %get-tuple-element.56.kept, ...), custom_call_target="tpu_custom_call" | custom-call | tf_op jit(solution)/shard_map/second_kernel/pallas_call | solution.py:413
  37.1 0.1 collective-permute-start.10
  37.2 1.1 %collective-permute-start.11 = (f32[8,32,128]{2,1,0:T(8,128)S(1)}, f32[8,32,128]{2,1,0:T(8,128)S(1)}, u32[]{:S(2)}, u32[]{:S(2)}) collective-permute-start(f32[8,32,128]{2,1,0:T(8,128)S(1)} %get-tuple-element.58), channel_id=1, source_target_pairs={{0,1},{2,3},{4,5},{6,7},{8,9},{10,11},{12,13},{14,15},{16,17},{18,... | collective-permute-start | bytes 393224 | tf_op jit(solution)/shard_map/ppermute | solution.py:443
  38.3 5.0 %collective-permute-done.10.first = f32[8,32,128]{2,1,0:T(8,128)S(1)} collective-permute-done((f32[8,32,128]{2,1,0:T(8,128)S(1)}, f32[8,32,128]{2,1,0:T(8,128)S(1)}, u32[]{:S(2)}, u32[]{:S(2)}) %collective-permute-start.10) | collective-permute-done | bytes 131104 | tf_op jit(solution)/shard_map/ppermute | solution.py:443
  43.3 2.8 %last_kernel.1 = f32[12,8,1024]{2,1,0:T(8,128)} custom-call(f32[352,128]{1,0:T(8,128)S(1)} %collective-permute-done.6.trace_first, f32[352,128]{1,0:T(8,128)S(1)} %collective-permute-done.7.trace_second, f32[8,32,128]{2,1,0:T(8,128)S(1)} %collective-permute-done.10.first, f32[8,32,128]{2,1,0:T(8,128)S(1)} %collective-permute-done.11.second, ...), custom_call_target="tpu_custom_call" | custom-call | tf_op jit(solution)/shard_map/last_kernel/pallas_call | solution.py:413
  (19 shorter events, 0.1 us)
Async XLA Ops:
  0.0 6.9 %copy-start.1 = (f32[12,8,1024]{2,1,0:T(8,128)S(1)}, f32[12,8,1024]{2,1,0:T(8,128)}, u32[]{:S(2)}) copy-start(f32[12,8,1024]{2,1,0:T(8,128)} %diffusivity.3) | copy-start | bytes 1179652
  0.0 6.9 %copy-start = (f32[12,8,1024]{2,1,0:T(8,128)S(1)}, f32[12,8,1024]{2,1,0:T(8,128)}, u32[]{:S(2)}) copy-start(f32[12,8,1024]{2,1,0:T(8,128)} %start_field.3) | copy-start | bytes 1179652
  1.4 11.6 %collective-permute-start = (f32[672,128]{1,0:T(8,128)S(1)}, f32[672,128]{1,0:T(8,128)S(1)}, u32[]{:S(2)}, u32[]{:S(2)}) collective-permute-start(f32[672,128]{1,0:T(8,128)S(1)} %get-tuple-element.33), channel_id=1, source_target_pairs={{1,2},{3,4},{5,6},{7,8},{9,10},{11,12},{13,14},{0,64},{15,79},{17,... | collective-permute-start | bytes 1032200 | tf_op jit(solution)/shard_map/ppermute | solution.py:443
  3.1 9.9 %collective-permute-start.1 = (f32[672,128]{1,0:T(8,128)S(1)}, f32[672,128]{1,0:T(8,128)S(1)}, u32[]{:S(2)}, u32[]{:S(2)}) collective-permute-start(f32[672,128]{1,0:T(8,128)S(1)} %get-tuple-element.34), channel_id=1, source_target_pairs={{0,1},{2,3},{4,5},{6,7},{8,9},{10,11},{12,13},{14,15},{16,17},{18,... | collective-permute-start | bytes 1032200 | tf_op jit(solution)/shard_map/ppermute | solution.py:443
  3.5 0.8 %copy-start.2 = (s32[12,8,16]{2,1,0:T(8,128)S(1)}, s32[12,8,16]{2,1,0:T(8,128)}, u32[]{:S(2)}) copy-start(s32[12,8,16]{2,1,0:T(8,128)} %tile_block.1) | copy-start | bytes 18436
  4.3 0.7 %copy-start.3 = (s32[4096]{0:T(1024)S(1)}, s32[4096]{0:T(1024)}, u32[]{:S(2)}) copy-start(s32[4096]{0:T(1024)} %param.8) | copy-start | bytes 49156
  5.1 7.9 %collective-permute-start.2 = (f32[40,128]{1,0:T(8,128)S(1)}, f32[40,128]{1,0:T(8,128)S(1)}, u32[]{:S(2)}, u32[]{:S(2)}) collective-permute-start(f32[40,128]{1,0:T(8,128)S(1)} %get-tuple-element.35), channel_id=1, source_target_pairs={{1,2},{3,4},{5,6},{7,8},{9,10},{11,12},{13,14},{0,64},{15,79},{17,... | collective-permute-start | bytes 61448 | tf_op jit(solution)/shard_map/ppermute | solution.py:443
  5.8 7.2 %collective-permute-start.3 = (f32[40,128]{1,0:T(8,128)S(1)}, f32[40,128]{1,0:T(8,128)S(1)}, u32[]{:S(2)}, u32[]{:S(2)}) collective-permute-start(f32[40,128]{1,0:T(8,128)S(1)} %get-tuple-element.36), channel_id=1, source_target_pairs={{0,1},{2,3},{4,5},{6,7},{8,9},{10,11},{12,13},{14,15},{16,17},{18,... | collective-permute-start | bytes 61448 | tf_op jit(solution)/shard_map/ppermute | solution.py:443
  14.8 9.1 %collective-permute-start.4 = (f32[272,128]{1,0:T(8,128)S(1)}, f32[272,128]{1,0:T(8,128)S(1)}, u32[]{:S(2)}, u32[]{:S(2)}) collective-permute-start(f32[272,128]{1,0:T(8,128)S(1)} %get-tuple-element.44), channel_id=1, source_target_pairs={{1,2},{3,4},{5,6},{7,8},{9,10},{11,12},{13,14},{0,64},{15,79},{17,... | collective-permute-start | bytes 417800 | tf_op jit(solution)/shard_map/ppermute | solution.py:443
  16.4 7.5 %collective-permute-start.5 = (f32[272,128]{1,0:T(8,128)S(1)}, f32[272,128]{1,0:T(8,128)S(1)}, u32[]{:S(2)}, u32[]{:S(2)}) collective-permute-start(f32[272,128]{1,0:T(8,128)S(1)} %get-tuple-element.45), channel_id=1, source_target_pairs={{0,1},{2,3},{4,5},{6,7},{8,9},{10,11},{12,13},{14,15},{16,17},{18,... | collective-permute-start | bytes 417800 | tf_op jit(solution)/shard_map/ppermute | solution.py:443
  16.4 19.7 %collective-permute-start.8 = (f32[352,128]{1,0:T(8,128)S(1)}, f32[352,128]{1,0:T(8,128)S(1)}, u32[]{:S(2)}, u32[]{:S(2)}) collective-permute-start(f32[352,128]{1,0:T(8,128)S(1)} %get-tuple-element.54), channel_id=1, source_target_pairs={{16,32},{48,64},{80,96},{112,128},{144,160},{176,192},{208,224},{0... | collective-permute-start | bytes 540680 | tf_op jit(solution)/shard_map/ppermute | solution.py:443
  21.9 14.1 %collective-permute-start.9 = (f32[352,128]{1,0:T(8,128)S(1)}, f32[352,128]{1,0:T(8,128)S(1)}, u32[]{:S(2)}, u32[]{:S(2)}) collective-permute-start(f32[352,128]{1,0:T(8,128)S(1)} %get-tuple-element.55), channel_id=1, source_target_pairs={{0,16},{32,48},{64,80},{96,112},{128,144},{160,176},{192,208},{224... | collective-permute-start | bytes 540680 | tf_op jit(solution)/shard_map/ppermute | solution.py:443
  24.6 18.6 %collective-permute-start.6 = (f32[352,128]{1,0:T(8,128)S(1)}, f32[352,128]{1,0:T(8,128)S(1)}, u32[]{:S(2)}, u32[]{:S(2)}) collective-permute-start(f32[352,128]{1,0:T(8,128)S(1)} %get-tuple-element.52), channel_id=1, source_target_pairs={{16,32},{48,64},{80,96},{112,128},{144,160},{176,192},{208,224},{0... | collective-permute-start | bytes 540680 | tf_op jit(solution)/shard_map/ppermute | solution.py:443
  30.7 12.6 %collective-permute-start.7 = (f32[352,128]{1,0:T(8,128)S(1)}, f32[352,128]{1,0:T(8,128)S(1)}, u32[]{:S(2)}, u32[]{:S(2)}) collective-permute-start(f32[352,128]{1,0:T(8,128)S(1)} %get-tuple-element.53), channel_id=1, source_target_pairs={{0,16},{32,48},{64,80},{96,112},{128,144},{160,176},{192,208},{224... | collective-permute-start | bytes 540680 | tf_op jit(solution)/shard_map/ppermute | solution.py:443
  37.1 6.2 %collective-permute-start.10 = (f32[8,32,128]{2,1,0:T(8,128)S(1)}, f32[8,32,128]{2,1,0:T(8,128)S(1)}, u32[]{:S(2)}, u32[]{:S(2)}) collective-permute-start(f32[8,32,128]{2,1,0:T(8,128)S(1)} %get-tuple-element.57), channel_id=1, source_target_pairs={{1,2},{3,4},{5,6},{7,8},{9,10},{11,12},{13,14},{0,64},{15,79},{17,... | collective-permute-start | bytes 393224 | tf_op jit(solution)/shard_map/ppermute | solution.py:443
  37.2 6.1 %collective-permute-start.11 = (f32[8,32,128]{2,1,0:T(8,128)S(1)}, f32[8,32,128]{2,1,0:T(8,128)S(1)}, u32[]{:S(2)}, u32[]{:S(2)}) collective-permute-start(f32[8,32,128]{2,1,0:T(8,128)S(1)} %get-tuple-element.58), channel_id=1, source_target_pairs={{0,1},{2,3},{4,5},{6,7},{8,9},{10,11},{12,13},{14,15},{16,17},{18,... | collective-permute-start | bytes 393224 | tf_op jit(solution)/shard_map/ppermute | solution.py:443

commit v4 on v3

--- a/solution.py
+++ b/solution.py
@@ -276,7 +276,7 @@
         low, high = reach(level)
         ghosts(src, low, high)
         for outer in (low, high - SIDE):
-            advance(src, dst, factor, marks, weight, 0, PLANES, outer, outer + SIDE)
+            advance_groups(src, dst, factor, marks, weight, 2, 6, 6, outer, outer + SIDE)
         if level < SIDE - 1:
             inner = (inner_1, inner_2, inner_3)[level]
             dst[1 : PLANES + 1, span(low + SIDE, high - SIDE), :] = inner[...]

time: 46.7 us -> 46.8 us (level)
  no operation moved by 1% of the time
where the time goes in v4:
time: 46.8 us; the launch traced here: 46.2 us
  starting transfers between devices  19.6 us (42%)
  waiting for transfers between devices  14.5 us (31%)
  Pallas kernels  9.47 us (20%)
  local copies, waits for them, and re-layouts  2.45 us (5%)
    ppermute x12, starting transfers between devices, swap(): lax.ppermute(cells, ('zg', 'xy'), pairing + [(j, i) for i, j in pairing])  19.6 us
    ppermute x12, waiting for transfers between devices, swap(): lax.ppermute(cells, ('zg', 'xy'), pairing + [(j, i) for i, j in pairing])  14.5 us
    pallas_call x8, Pallas kernels, call(): pl.pallas_call(kernel, out_shape=[shape(*dims) for dims in outs], in_spec...  9.47 us
    unnamed x9, local copies, waits for them, and re-layouts  2.44 us
  transfers between devices with their start and end apart: 12, of which 3 were waited for; matrix products, arithmetic and copies ran while one was open for 2% of the time, Pallas kernels for 7%

profile of v4, /device:TPU:30, one launch (start us, length us, event | category | flops | bytes accessed | tf_op | source)
XLA Modules:
  0.0 46.2 jit_solution(15620433728430804976)
XLA Ops:
  0.0 1.4 %prepare_kernel.1 = (f32[672,128]{1,0:T(8,128)S(1)}, f32[672,128]{1,0:T(8,128)S(1)}) custom-call(f32[12,8,1024]{2,1,0:T(8,128)} %start_field.3, f32[12,8,1024]{2,1,0:T(8,128)} %diffusivity.3), custom_call_target="tpu_custom_call" | custom-call | tf_op jit(solution)/shard_map/prepare_kernel/pallas_call | solution.py:413
  1.4 1.7 %collective-permute-start = (f32[672,128]{1,0:T(8,128)S(1)}, f32[672,128]{1,0:T(8,128)S(1)}, u32[]{:S(2)}, u32[]{:S(2)}) collective-permute-start(f32[672,128]{1,0:T(8,128)S(1)} %get-tuple-element.33), channel_id=1, source_target_pairs={{1,2},{3,4},{5,6},{7,8},{9,10},{11,12},{13,14},{0,64},{15,79},{17,... | collective-permute-start | bytes 1032200 | tf_op jit(solution)/shard_map/ppermute | solution.py:443
  3.1 0.4 collective-permute-start.1
  3.5 0.8 %copy-done.2 = s32[12,8,16]{2,1,0:T(8,128)S(1)} copy-done((s32[12,8,16]{2,1,0:T(8,128)S(1)}, s32[12,8,16]{2,1,0:T(8,128)}, u32[]{:S(2)}) %copy-start.2) | copy-done | bytes 6168
  4.3 0.7 %copy-done.3 = s32[4096]{0:T(1024)S(1)} copy-done((s32[4096]{0:T(1024)S(1)}, s32[4096]{0:T(1024)}, u32[]{:S(2)}) %copy-start.3) | copy-done | bytes 16408
  5.0 0.1 code_kernel.1
  5.1 0.7 %collective-permute-start.2 = (f32[40,128]{1,0:T(8,128)S(1)}, f32[40,128]{1,0:T(8,128)S(1)}, u32[]{:S(2)}, u32[]{:S(2)}) collective-permute-start(f32[40,128]{1,0:T(8,128)S(1)} %get-tuple-element.35), channel_id=1, source_target_pairs={{1,2},{3,4},{5,6},{7,8},{9,10},{11,12},{13,14},{0,64},{15,79},{17,... | collective-permute-start | bytes 61448 | tf_op jit(solution)/shard_map/ppermute | solution.py:443
  5.9 0.9 %copy.6 = f32[2,64,64]{1,2,0:T(8,128)S(1)} copy(f32[2,64,64]{2,1,0:T(8,128)} %param.9) | data formatting | bytes 65536 | tf_op args[4]
  6.9 0.9 %own_kernel.1 = (f32[12,64,128]{2,1,0:T(8,128)S(1)}, f32[12,192,128]{2,1,0:T(8,128)S(1)}, f32[12,192,128]{2,1,0:T(8,128)S(1)}, f32[12,48,128]{2,1,0:T(8,128)S(1)...) custom-call(f32[12,8,1024]{2,1,0:T(8,128)S(1)} %copy-done, f32[12,8,1024]{2,1,0:T(8,128)S(1)} %copy-done.1, ...), custom_call_target="tpu_custom_call" | custom-call | tf_op jit(solution)/shard_map/own_kernel/pallas_call | solution.py:413
  7.8 5.2 %collective-permute-done.2.code_first = f32[40,128]{1,0:T(8,128)S(1)} collective-permute-done((f32[40,128]{1,0:T(8,128)S(1)}, f32[40,128]{1,0:T(8,128)S(1)}, u32[]{:S(2)}, u32[]{:S(2)}) %collective-permute-start.2) | collective-permute-done | bytes 20512 | tf_op jit(solution)/shard_map/ppermute | solution.py:443
  13.0 1.8 %first_kernel.1 = (f32[272,128]{1,0:T(8,128)S(1)}, f32[272,128]{1,0:T(8,128)S(1)}, f32[352,128]{1,0:T(8,128)S(1)}, f32[352,128]{1,0:T(8,128)S(1)}, f32[12,64,128...) custom-call(f32[672,128]{1,0:T(8,128)S(1)} %collective-permute-done.near, ...), custom_call_target="tpu_custom_call" | custom-call | tf_op jit(solution)/shard_map/first_kernel/pallas_call | solution.py:413
  14.9 1.6 %collective-permute-start.4 = (f32[272,128]{1,0:T(8,128)S(1)}, f32[272,128]{1,0:T(8,128)S(1)}, u32[]{:S(2)}, u32[]{:S(2)}) collective-permute-start(f32[272,128]{1,0:T(8,128)S(1)} %get-tuple-element.44), channel_id=1, source_target_pairs={{1,2},{3,4},{5,6},{7,8},{9,10},{11,12},{13,14},{0,64},{15,79},{17,... | collective-permute-start | bytes 417800 | tf_op jit(solution)/shard_map/ppermute | solution.py:443
  16.5 5.6 %collective-permute-start.8 = (f32[352,128]{1,0:T(8,128)S(1)}, f32[352,128]{1,0:T(8,128)S(1)}, u32[]{:S(2)}, u32[]{:S(2)}) collective-permute-start(f32[352,128]{1,0:T(8,128)S(1)} %get-tuple-element.54), channel_id=1, source_target_pairs={{16,32},{48,64},{80,96},{112,128},{144,160},{176,192},{208,224},{0... | collective-permute-start | bytes 540680 | tf_op jit(solution)/shard_map/ppermute | solution.py:443
  22.0 1.3 %collective-permute-start.9 = (f32[352,128]{1,0:T(8,128)S(1)}, f32[352,128]{1,0:T(8,128)S(1)}, u32[]{:S(2)}, u32[]{:S(2)}) collective-permute-start(f32[352,128]{1,0:T(8,128)S(1)} %get-tuple-element.55), channel_id=1, source_target_pairs={{0,16},{32,48},{64,80},{96,112},{128,144},{160,176},{192,208},{224... | collective-permute-start | bytes 540680 | tf_op jit(solution)/shard_map/ppermute | solution.py:443
  23.3 0.7 %inner_kernel.1 = (f32[12,48,128]{2,1,0:T(8,128)S(1)}, f32[12,32,128]{2,1,0:T(8,128)S(1)}, f32[12,16,128]{2,1,0:T(8,128)S(1)}) custom-call(f32[12,64,128]{2,1,0:T(8,128)S(1)} %get-tuple-element.46.state, f32[12,192,128]{2,1,0:T(8,128)S(1)} %get-tuple-element.47.factor, f32[12,192,128]{2,1,0:T(8,128)S(1)} %get-tuple-element.48.marks, f32[128,256]{1,0:T(8,128)S(1)} %fusion.couple), custom_call_target="tpu_custom_call" | custom-call | tf_op jit(solution)/shard_map/inner_kernel/pallas_call | solution.py:413
  24.0 0.7 %middle_kernel.1 = (f32[352,128]{1,0:T(8,128)S(1)}, f32[352,128]{1,0:T(8,128)S(1)}, f32[6,192,128]{2,1,0:T(8,128)S(1)}) custom-call(f32[272,128]{1,0:T(8,128)S(1)} %collective-permute-done.4.first, f32[272,128]{1,0:T(8,128)S(1)} %collective-permute-done.5.second, f32[12,64,128]{2,1,0:T(8,128)S(1)} %get-tuple-element.46.state, ...), custom_call_target="tpu_custom_call" | custom-call | tf_op jit(solution)/shard_map/middle_kernel/pallas_call | solution.py:413
  24.7 6.1 %collective-permute-start.6 = (f32[352,128]{1,0:T(8,128)S(1)}, f32[352,128]{1,0:T(8,128)S(1)}, u32[]{:S(2)}, u32[]{:S(2)}) collective-permute-start(f32[352,128]{1,0:T(8,128)S(1)} %get-tuple-element.52), channel_id=1, source_target_pairs={{16,32},{48,64},{80,96},{112,128},{144,160},{176,192},{208,224},{0... | collective-permute-start | bytes 540680 | tf_op jit(solution)/shard_map/ppermute | solution.py:443
  30.8 1.1 %collective-permute-start.7 = (f32[352,128]{1,0:T(8,128)S(1)}, f32[352,128]{1,0:T(8,128)S(1)}, u32[]{:S(2)}, u32[]{:S(2)}) collective-permute-start(f32[352,128]{1,0:T(8,128)S(1)} %get-tuple-element.53), channel_id=1, source_target_pairs={{0,16},{32,48},{64,80},{96,112},{128,144},{160,176},{192,208},{224... | collective-permute-start | bytes 540680 | tf_op jit(solution)/shard_map/ppermute | solution.py:443
  31.9 4.3 %collective-permute-done.8.trace_first = f32[352,128]{1,0:T(8,128)S(1)} collective-permute-done((f32[352,128]{1,0:T(8,128)S(1)}, f32[352,128]{1,0:T(8,128)S(1)}, u32[]{:S(2)}, u32[]{:S(2)}) %collective-permute-start.8) | collective-permute-done | bytes 180256 | tf_op jit(solution)/shard_map/ppermute | solution.py:443
  36.2 1.0 %second_kernel.1 = (f32[8,32,128]{2,1,0:T(8,128)S(1)}, f32[8,32,128]{2,1,0:T(8,128)S(1)}, f32[8,64,128]{2,1,0:T(8,128)S(1)}) custom-call(f32[352,128]{1,0:T(8,128)S(1)} %collective-permute-done.8.trace_first, f32[352,128]{1,0:T(8,128)S(1)} %collective-permute-done.9.trace_second, f32[16,192,128]{2,1,0:T(8,128)S(1)} %get-tuple-element.56.kept, ...), custom_call_target="tpu_custom_call" | custom-call | tf_op jit(solution)/shard_map/second_kernel/pallas_call | solution.py:413
  37.2 0.1 collective-permute-start.10
  37.3 1.1 %collective-permute-start.11 = (f32[8,32,128]{2,1,0:T(8,128)S(1)}, f32[8,32,128]{2,1,0:T(8,128)S(1)}, u32[]{:S(2)}, u32[]{:S(2)}) collective-permute-start(f32[8,32,128]{2,1,0:T(8,128)S(1)} %get-tuple-element.58), channel_id=1, source_target_pairs={{0,1},{2,3},{4,5},{6,7},{8,9},{10,11},{12,13},{14,15},{16,17},{18,... | collective-permute-start | bytes 393224 | tf_op jit(solution)/shard_map/ppermute | solution.py:443
  38.4 5.0 %collective-permute-done.10.first = f32[8,32,128]{2,1,0:T(8,128)S(1)} collective-permute-done((f32[8,32,128]{2,1,0:T(8,128)S(1)}, f32[8,32,128]{2,1,0:T(8,128)S(1)}, u32[]{:S(2)}, u32[]{:S(2)}) %collective-permute-start.10) | collective-permute-done | bytes 131104 | tf_op jit(solution)/shard_map/ppermute | solution.py:443
  43.4 2.8 %last_kernel.1 = f32[12,8,1024]{2,1,0:T(8,128)} custom-call(f32[352,128]{1,0:T(8,128)S(1)} %collective-permute-done.6.trace_first, f32[352,128]{1,0:T(8,128)S(1)} %collective-permute-done.7.trace_second, f32[8,32,128]{2,1,0:T(8,128)S(1)} %collective-permute-done.10.first, f32[8,32,128]{2,1,0:T(8,128)S(1)} %collective-permute-done.11.second, ...), custom_call_target="tpu_custom_call" | custom-call | tf_op jit(solution)/shard_map/last_kernel/pallas_call | solution.py:413
  (19 shorter events, 0.1 us)
Async XLA Ops:
  0.0 6.9 %copy-start.1 = (f32[12,8,1024]{2,1,0:T(8,128)S(1)}, f32[12,8,1024]{2,1,0:T(8,128)}, u32[]{:S(2)}) copy-start(f32[12,8,1024]{2,1,0:T(8,128)} %diffusivity.3) | copy-start | bytes 1179652
  0.0 6.9 %copy-start = (f32[12,8,1024]{2,1,0:T(8,128)S(1)}, f32[12,8,1024]{2,1,0:T(8,128)}, u32[]{:S(2)}) copy-start(f32[12,8,1024]{2,1,0:T(8,128)} %start_field.3) | copy-start | bytes 1179652
  1.4 11.6 %collective-permute-start = (f32[672,128]{1,0:T(8,128)S(1)}, f32[672,128]{1,0:T(8,128)S(1)}, u32[]{:S(2)}, u32[]{:S(2)}) collective-permute-start(f32[672,128]{1,0:T(8,128)S(1)} %get-tuple-element.33), channel_id=1, source_target_pairs={{1,2},{3,4},{5,6},{7,8},{9,10},{11,12},{13,14},{0,64},{15,79},{17,... | collective-permute-start | bytes 1032200 | tf_op jit(solution)/shard_map/ppermute | solution.py:443
  3.1 9.9 %collective-permute-start.1 = (f32[672,128]{1,0:T(8,128)S(1)}, f32[672,128]{1,0:T(8,128)S(1)}, u32[]{:S(2)}, u32[]{:S(2)}) collective-permute-start(f32[672,128]{1,0:T(8,128)S(1)} %get-tuple-element.34), channel_id=1, source_target_pairs={{0,1},{2,3},{4,5},{6,7},{8,9},{10,11},{12,13},{14,15},{16,17},{18,... | collective-permute-start | bytes 1032200 | tf_op jit(solution)/shard_map/ppermute | solution.py:443
  3.5 0.8 %copy-start.2 = (s32[12,8,16]{2,1,0:T(8,128)S(1)}, s32[12,8,16]{2,1,0:T(8,128)}, u32[]{:S(2)}) copy-start(s32[12,8,16]{2,1,0:T(8,128)} %tile_block.1) | copy-start | bytes 18436
  4.3 0.7 %copy-start.3 = (s32[4096]{0:T(1024)S(1)}, s32[4096]{0:T(1024)}, u32[]{:S(2)}) copy-start(s32[4096]{0:T(1024)} %param.8) | copy-start | bytes 49156
  5.1 7.9 %collective-permute-start.2 = (f32[40,128]{1,0:T(8,128)S(1)}, f32[40,128]{1,0:T(8,128)S(1)}, u32[]{:S(2)}, u32[]{:S(2)}) collective-permute-start(f32[40,128]{1,0:T(8,128)S(1)} %get-tuple-element.35), channel_id=1, source_target_pairs={{1,2},{3,4},{5,6},{7,8},{9,10},{11,12},{13,14},{0,64},{15,79},{17,... | collective-permute-start | bytes 61448 | tf_op jit(solution)/shard_map/ppermute | solution.py:443
  5.8 7.2 %collective-permute-start.3 = (f32[40,128]{1,0:T(8,128)S(1)}, f32[40,128]{1,0:T(8,128)S(1)}, u32[]{:S(2)}, u32[]{:S(2)}) collective-permute-start(f32[40,128]{1,0:T(8,128)S(1)} %get-tuple-element.36), channel_id=1, source_target_pairs={{0,1},{2,3},{4,5},{6,7},{8,9},{10,11},{12,13},{14,15},{16,17},{18,... | collective-permute-start | bytes 61448 | tf_op jit(solution)/shard_map/ppermute | solution.py:443
  14.9 9.1 %collective-permute-start.4 = (f32[272,128]{1,0:T(8,128)S(1)}, f32[272,128]{1,0:T(8,128)S(1)}, u32[]{:S(2)}, u32[]{:S(2)}) collective-permute-start(f32[272,128]{1,0:T(8,128)S(1)} %get-tuple-element.44), channel_id=1, source_target_pairs={{1,2},{3,4},{5,6},{7,8},{9,10},{11,12},{13,14},{0,64},{15,79},{17,... | collective-permute-start | bytes 417800 | tf_op jit(solution)/shard_map/ppermute | solution.py:443
  16.5 7.5 %collective-permute-start.5 = (f32[272,128]{1,0:T(8,128)S(1)}, f32[272,128]{1,0:T(8,128)S(1)}, u32[]{:S(2)}, u32[]{:S(2)}) collective-permute-start(f32[272,128]{1,0:T(8,128)S(1)} %get-tuple-element.45), channel_id=1, source_target_pairs={{0,1},{2,3},{4,5},{6,7},{8,9},{10,11},{12,13},{14,15},{16,17},{18,... | collective-permute-start | bytes 417800 | tf_op jit(solution)/shard_map/ppermute | solution.py:443
  16.5 19.7 %collective-permute-start.8 = (f32[352,128]{1,0:T(8,128)S(1)}, f32[352,128]{1,0:T(8,128)S(1)}, u32[]{:S(2)}, u32[]{:S(2)}) collective-permute-start(f32[352,128]{1,0:T(8,128)S(1)} %get-tuple-element.54), channel_id=1, source_target_pairs={{16,32},{48,64},{80,96},{112,128},{144,160},{176,192},{208,224},{0... | collective-permute-start | bytes 540680 | tf_op jit(solution)/shard_map/ppermute | solution.py:443
  22.0 14.1 %collective-permute-start.9 = (f32[352,128]{1,0:T(8,128)S(1)}, f32[352,128]{1,0:T(8,128)S(1)}, u32[]{:S(2)}, u32[]{:S(2)}) collective-permute-start(f32[352,128]{1,0:T(8,128)S(1)} %get-tuple-element.55), channel_id=1, source_target_pairs={{0,16},{32,48},{64,80},{96,112},{128,144},{160,176},{192,208},{224... | collective-permute-start | bytes 540680 | tf_op jit(solution)/shard_map/ppermute | solution.py:443
  24.7 18.6 %collective-permute-start.6 = (f32[352,128]{1,0:T(8,128)S(1)}, f32[352,128]{1,0:T(8,128)S(1)}, u32[]{:S(2)}, u32[]{:S(2)}) collective-permute-start(f32[352,128]{1,0:T(8,128)S(1)} %get-tuple-element.52), channel_id=1, source_target_pairs={{16,32},{48,64},{80,96},{112,128},{144,160},{176,192},{208,224},{0... | collective-permute-start | bytes 540680 | tf_op jit(solution)/shard_map/ppermute | solution.py:443
  30.8 12.6 %collective-permute-start.7 = (f32[352,128]{1,0:T(8,128)S(1)}, f32[352,128]{1,0:T(8,128)S(1)}, u32[]{:S(2)}, u32[]{:S(2)}) collective-permute-start(f32[352,128]{1,0:T(8,128)S(1)} %get-tuple-element.53), channel_id=1, source_target_pairs={{0,16},{32,48},{64,80},{96,112},{128,144},{160,176},{192,208},{224... | collective-permute-start | bytes 540680 | tf_op jit(solution)/shard_map/ppermute | solution.py:443
  37.2 6.2 %collective-permute-start.10 = (f32[8,32,128]{2,1,0:T(8,128)S(1)}, f32[8,32,128]{2,1,0:T(8,128)S(1)}, u32[]{:S(2)}, u32[]{:S(2)}) collective-permute-start(f32[8,32,128]{2,1,0:T(8,128)S(1)} %get-tuple-element.57), channel_id=1, source_target_pairs={{1,2},{3,4},{5,6},{7,8},{9,10},{11,12},{13,14},{0,64},{15,79},{17,... | collective-permute-start | bytes 393224 | tf_op jit(solution)/shard_map/ppermute | solution.py:443
  37.3 6.1 %collective-permute-start.11 = (f32[8,32,128]{2,1,0:T(8,128)S(1)}, f32[8,32,128]{2,1,0:T(8,128)S(1)}, u32[]{:S(2)}, u32[]{:S(2)}) collective-permute-start(f32[8,32,128]{2,1,0:T(8,128)S(1)} %get-tuple-element.58), channel_id=1, source_target_pairs={{0,1},{2,3},{4,5},{6,7},{8,9},{10,11},{12,13},{14,15},{16,17},{18,... | collective-permute-start | bytes 393224 | tf_op jit(solution)/shard_map/ppermute | solution.py:443
